TPU v7x, 256 devices: a whole 4x4x8 slice. The times are simulated.
256 devices in a mesh: frame: 16 (over z_lo, y), token: 8 (over x, core), dp: 2 (over z_hi).
Axes of the slice: x: 4, y: 4, z: 8 (z_hi: 2, z_lo: 4; z = z_hi * 4 + z_lo), core: 2. Of those that a mesh axis runs over, the one named last changes fastest.
Arguments:
- temporal_qkv: bfloat16 [3, 2, 128, 128, 1024], P(None, 'dp', 'frame', 'token'), may hold values from -6 to 6
- spatial_qkv: bfloat16 [3, 2, 128, 128, 1024], P(None, 'dp', 'frame', 'token'), may hold values from -6 to 6
- out_grad: bfloat16 [2, 128, 128, 1024], P('dp', 'frame', 'token'), may hold values from -6 to 6
- temporal_proj: bfloat16 [1024, 1024], replicated, may hold values from -0.1875 to 0.1875
- spatial_proj: bfloat16 [1024, 1024], replicated, may hold values from -0.1875 to 0.1875
Outputs:
- temporal_qkv_grad: bfloat16 [3, 2, 128, 128, 1024], P(None, 'dp', 'frame', 'token')
- spatial_qkv_grad: bfloat16 [3, 2, 128, 128, 1024], P(None, 'dp', 'frame', 'token')
- temporal_proj_grad: float32 [1024, 1024], P('frame', ('token', 'dp'))
- spatial_proj_grad: float32 [1024, 1024], P('frame', ('token', 'dp'))
All inputs are finite; a program needn't handle non-finite values.
Results may differ from a plain program's by a relative error of at most 0.025.
Values may be sent and summed in bfloat16 or wider, within the bound.
A program may use at most 128 MiB of HBM per device.

v0:
```python
import jax
import jax.numpy as jnp
from jax import lax
from jax.sharding import PartitionSpec as P

HEADS = 16


def project(cotangent, projection):
    flat_rows = cotangent.reshape(-1, cotangent.shape[-1])
    result = jnp.dot(flat_rows, projection, preferred_element_type=jnp.float32)
    return result.astype(jnp.bfloat16).reshape(cotangent.shape)


def attend(qkv_block, branch_grad, temporal):
    grid_shape = branch_grad.shape
    head_shape = grid_shape[:3] + (HEADS, grid_shape[3] // HEADS)
    inv_root = (grid_shape[3] // HEADS) ** (-0.5)
    query_h = qkv_block[0].reshape(head_shape)
    key_h = qkv_block[1].reshape(head_shape)
    value_h = qkv_block[2].reshape(head_shape)
    upstream = branch_grad.reshape(head_shape)
    row_spec = "cibhe" if temporal else "cbihe"
    col_spec = "cjbhe" if temporal else "cbjhe"
    pair_spec = "cbhij"
    scores = (
        jnp.einsum(
            row_spec + "," + col_spec + "->" + pair_spec,
            query_h,
            key_h,
            preferred_element_type=jnp.float32,
        )
        * inv_root
    )
    attn_probs = jax.nn.softmax(scores, axis=-1)
    probs_low = attn_probs.astype(jnp.bfloat16)
    attn_out = jnp.einsum(
        pair_spec + "," + col_spec + "->" + row_spec,
        probs_low,
        value_h,
        preferred_element_type=jnp.float32,
    ).astype(jnp.bfloat16)
    prob_grad = jnp.einsum(
        row_spec + "," + col_spec + "->" + pair_spec,
        upstream,
        value_h,
        preferred_element_type=jnp.float32,
    )
    row_delta = jnp.einsum(
        row_spec + "," + row_spec + "->cbhi", upstream, attn_out, preferred_element_type=jnp.float32
    )
    score_grad = (attn_probs * (prob_grad - row_delta[..., None])).astype(jnp.bfloat16)
    query_grad = (
        jnp.einsum(
            pair_spec + "," + col_spec + "->" + row_spec,
            score_grad,
            key_h,
            preferred_element_type=jnp.float32,
        )
        * inv_root
    ).astype(jnp.bfloat16)
    key_grad = (
        jnp.einsum(
            pair_spec + "," + row_spec + "->" + col_spec,
            score_grad,
            query_h,
            preferred_element_type=jnp.float32,
        )
        * inv_root
    ).astype(jnp.bfloat16)
    value_grad = jnp.einsum(
        pair_spec + "," + row_spec + "->" + col_spec,
        probs_low,
        upstream,
        preferred_element_type=jnp.float32,
    ).astype(jnp.bfloat16)
    stacked = jnp.stack([query_grad, key_grad, value_grad]).reshape((3,) + grid_shape)
    return (attn_out.reshape(grid_shape), stacked)


def local(temporal_qkv, spatial_qkv, out_grad, temporal_proj, spatial_proj):
    width = out_grad.shape[-1]
    temporal_extra = project(out_grad, temporal_proj)
    spatial_extra = project(out_grad, spatial_proj)
    temporal_send = jnp.concatenate([temporal_qkv, temporal_extra[None]], axis=0)
    spatial_send = jnp.concatenate([spatial_qkv, spatial_extra[None]], axis=0)
    temporal_recv = lax.all_to_all(temporal_send, "frame", split_axis=3, concat_axis=2, tiled=True)
    spatial_recv = lax.all_to_all(spatial_send, "token", split_axis=2, concat_axis=3, tiled=True)
    temporal_branch = temporal_recv[3]
    spatial_branch = spatial_recv[3]
    temporal_out, temporal_grads = attend(temporal_recv[:3], temporal_branch, True)
    spatial_out, spatial_grads = attend(spatial_recv[:3], spatial_branch, False)
    temporal_back = lax.all_to_all(
        jnp.concatenate([temporal_grads, temporal_out[None]], axis=0),
        "frame",
        split_axis=2,
        concat_axis=3,
        tiled=True,
    )
    spatial_back = lax.all_to_all(
        jnp.concatenate([spatial_grads, spatial_out[None]], axis=0),
        "token",
        split_axis=3,
        concat_axis=2,
        tiled=True,
    )
    temporal_home = temporal_back[:3]
    spatial_home = spatial_back[:3]
    grad_pairs = ((out_grad, temporal_back[3]), (out_grad, spatial_back[3]))
    flat_pairs = tuple(
        (
            (cotangent.reshape(-1, width), branch_out.reshape(-1, width))
            for cotangent, branch_out in grad_pairs
        )
    )
    row_share = width // lax.axis_size("frame")
    blocks = []
    for cotangent, branch_out in flat_pairs:
        blocks.append(
            jnp.einsum("rd,re->de", cotangent, branch_out, preferred_element_type=jnp.float32)
        )
    row_part = lax.psum_scatter(
        jnp.concatenate(blocks, axis=1), "frame", scatter_dimension=0, tiled=True
    )
    summed = lax.psum_scatter(
        row_part.reshape(row_share, 2, width), ("token", "dp"), scatter_dimension=2, tiled=True
    )
    return (temporal_home, spatial_home, summed[:, 0, :], summed[:, 1, :])


def solution(mesh):
    in_specs = (
        P(None, "dp", "frame", "token", None),
        P(None, "dp", "frame", "token", None),
        P("dp", "frame", "token", None),
        P(),
        P(),
    )
    out_specs = (
        P(None, "dp", "frame", "token", None),
        P(None, "dp", "frame", "token", None),
        P("frame", ("token", "dp")),
        P("frame", ("token", "dp")),
    )
    return jax.shard_map(local, mesh=mesh, in_specs=in_specs, out_specs=out_specs, check_vma=False)
```

profile of v0, /device:TPU:8, one launch (start us, length us, event | category | flops | bytes accessed | tf_op | source)
XLA Modules:
  0.0 336.5 jit_solution(15129163960219018995)
XLA Ops:
  7.2 1.6 copy-done
  8.8 1.4 convolution_convert_fusion.2
  10.2 1.1 pad_maximum_fusion.3
  11.3 4.3 %all-to-all-start.2 = ((bf16[4,1,8,16,1024]{4,3,1,0,2:T(8,128)(2,1)}), bf16[4,1,8,16,1024]{4,3,1,0,2:T(8,128)(2,1)S(1)}, u32[]{:S(2)}, u32[]{:S(2)}) async-start(bf16[4,1,8,16,1024]{4,3,1,0,2:T(8,128)(2,1)} %pad_maximum_fusion.3), calls=%async_computation.2 | async-start | bytes 2097152 | tf_op jit(solution)/shard_map/all_to_all | solution.py:88
  15.6 2.1 convolution_convert_fusion.5
  18.3 1.1 pad_maximum_fusion.1
  19.5 12.1 %all-to-all-done.2 = bf16[4,1,8,16,1024]{4,3,1,0,2:T(8,128)(2,1)S(1)} async-done(((bf16[4,1,8,16,1024]{4,3,1,0,2:T(8,128)(2,1)}), bf16[4,1,8,16,1024]{4,3,1,0,2:T(8,128)(2,1)S(1)}, u32[]{:S(2)}, u32[]{:S(2)}) %all-to-all-start.2) | async-done | bytes 1048608 | tf_op jit(solution)/shard_map/all_to_all | solution.py:88
  31.6 9.0 %all-to-all-start = ((bf16[4,1,8,16,1024]{4,2,1,0,3:T(8,128)(2,1)}), bf16[4,1,8,16,1024]{4,2,1,0,3:T(8,128)(2,1)S(1)}, u32[]{:S(2)}, u32[]{:S(2)}) async-start(bf16[4,1,8,16,1024]{4,2,1,0,3:T(8,128)(2,1)} %pad_maximum_fusion.1), calls=%async_computation | async-start | bytes 2097152 | tf_op jit(solution)/shard_map/all_to_all | solution.py:87
  40.6 0.8 fusion.24
  41.7 1.2 copy.216
  43.0 1.2 copy.255
  44.2 1.3 reshape.224
  47.6 1.5 fusion.28
  50.4 0.8 convolution_convert_fusion
  51.6 1.8 fusion.9
  53.4 1.0 fusion.12
  54.4 2.0 copy.227
  57.3 4.5 %pad_maximum_fusion.4 = bf16[4,1,1,128,1024]{4,0,2,1,3:T(4,128)(2,1)} fusion(bf16[1,1,1,128,1024]{4,0,2,1,3:T(2,128)(2,1)S(1)} %copy.230, bf16[1,1,1,128,1024]{4,0,2,1,3:T(2,128)(2,1)S(1)} %copy.229, bf16[1,1,1,128,1024]{4,0,2,1,3:T(2,128)(2,1)S(1)} %copy.228, bf16[1,1,1,128,1024]{4,0,2,1,3:T(2,128)(2,1)} %copy.227), kind=kLoop, calls=%fused_computation.34 | loop fusion | flops 4194304 | bytes 2097152 | tf_op jit(solution)/shard_map/concatenate | solution.py:101
  61.7 1.6 all-to-all-done
  63.3 1.0 copy-done.4
  64.4 3.7 %all-to-all-start.3 = ((bf16[4,1,1,128,1024]{4,0,2,1,3:T(4,128)(2,1)}), bf16[4,1,1,128,1024]{4,0,2,1,3:T(4,128)(2,1)S(1)}, u32[]{:S(2)}, u32[]{:S(2)}) async-start(bf16[4,1,1,128,1024]{4,0,2,1,3:T(4,128)(2,1)} %pad_maximum_fusion.4), calls=%async_computation.3 | async-start | bytes 2097152 | tf_op jit(solution)/shard_map/all_to_all | solution.py:100
  68.1 2.0 fusion.25
  70.4 1.2 copy.196
  71.7 1.2 copy.244
  72.9 1.3 reshape.219
  76.3 1.5 fusion.27
  77.9 1.5 convolution_convert_fusion.3
  80.6 1.3 copy.209
  81.9 1.8 fusion.8
  83.7 1.0 fusion.10
  84.7 2.0 copy.207
  87.6 4.5 %pad_maximum_fusion.2 = bf16[4,1,128,1,1024]{4,0,3,1,2:T(4,128)(2,1)} fusion(bf16[1,1,128,1,1024]{4,0,3,1,2:T(2,128)(2,1)S(1)} %copy.210, bf16[1,1,128,1,1024]{4,0,3,1,2:T(2,128)(2,1)S(1)} %copy.209, bf16[1,1,128,1,1024]{4,0,3,1,2:T(2,128)(2,1)S(1)} %copy.208, bf16[1,1,128,1,1024]{4,0,3,1,2:T(2,128)(2,1)} %copy.207), kind=kLoop, calls=%fused_computation.32 | loop fusion | flops 4194304 | bytes 2097152 | tf_op jit(solution)/shard_map/concatenate | solution.py:94
  92.0 7.9 %all-to-all-start.1 = ((bf16[4,1,128,1,1024]{4,0,3,1,2:T(4,128)(2,1)}), bf16[4,1,128,1,1024]{4,0,3,1,2:T(4,128)(2,1)}, u32[]{:S(2)}, u32[]{:S(2)}) async-start(bf16[4,1,128,1,1024]{4,0,3,1,2:T(4,128)(2,1)} %pad_maximum_fusion.2), calls=%async_computation.1 | async-start | bytes 2097152 | tf_op jit(solution)/shard_map/all_to_all | solution.py:93
  100.8 2.7 convolution_bitcast_fusion
  103.5 19.8 %all-to-all-done.1 = bf16[4,1,128,1,1024]{4,0,3,1,2:T(4,128)(2,1)} async-done(((bf16[4,1,128,1,1024]{4,0,3,1,2:T(4,128)(2,1)}), bf16[4,1,128,1,1024]{4,0,3,1,2:T(4,128)(2,1)}, u32[]{:S(2)}, u32[]{:S(2)}) %all-to-all-start.1) | async-done | bytes 1048608 | tf_op jit(solution)/shard_map/all_to_all | solution.py:93
  123.3 1.5 copy.275
  125.8 1.6 copy-done.2
  127.4 4.1 %pad_maximum_fusion = f32[1024,2048]{0,1:T(8,128)} fusion(f32[1024,1024]{0,1:T(8,128)S(1)} %copy-done.2, f32[1024,1024]{0,1:T(8,128)S(1)} %convolution_bitcast_fusion.1), kind=kLoop, calls=%fused_computation.2 | loop fusion | flops 2097152 | bytes 16777216 | tf_op jit(solution)/shard_map/concatenate | solution.py:123
  131.5 9.1 %copy.259 = f32[1024,2048]{1,0:T(8,128)} copy(f32[1024,2048]{0,1:T(8,128)} %pad_maximum_fusion) | data formatting | bytes 16777216
  140.7 107.0 %reduce-scatter.7.cloned.1.call-done = f32[64,2048]{1,0:T(8,128)} async-done(((f32[1024,2048]{1,0:T(8,128)}), f32[64,2048]{1,0:T(8,128)}) %reduce-scatter.7.cloned.1.call-update) | async-done | bytes 524304
  247.7 1.4 copy.260
  249.1 0.8 copy.274
  249.9 1.4 reshape.235
  251.3 1.2 copy.264
  252.5 1.2 slice_bitcast_fusion
  253.7 1.3 copy.235
  255.0 72.4 %reduce-scatter.9.cloned.1.call-done = f32[64,128]{1,0:T(8,128)} async-done(((f32[1024,128]{1,0:T(8,128)}), f32[64,128]{1,0:T(8,128)}) %reduce-scatter.9.cloned.1.call-update) | async-done | bytes 32784
  327.4 0.9 reshape.236
  (62 shorter events, 13.7 us)
Async XLA Ops:
  7.2 1.6 copy-start
  7.2 3.0 copy-start.7
  10.2 5.4 %copy-start.3 = (bf16[1,8,16,1024]{3,2,1,0:T(8,128)(2,1)S(1)}, bf16[1,8,16,1024]{3,2,1,0:T(8,128)(2,1)}, u32[]{:S(2)}) copy-start(bf16[1,8,16,1024]{3,2,1,0:T(8,128)(2,1)} %param.7) | copy-start | bytes 786436
  11.3 20.3 %all-to-all-start.2 = ((bf16[4,1,8,16,1024]{4,3,1,0,2:T(8,128)(2,1)}), bf16[4,1,8,16,1024]{4,3,1,0,2:T(8,128)(2,1)S(1)}, u32[]{:S(2)}, u32[]{:S(2)}) async-start(bf16[4,1,8,16,1024]{4,3,1,0,2:T(8,128)(2,1)} %pad_maximum_fusion.3), calls=%async_computation.2 | async-start | bytes 2097152 | tf_op jit(solution)/shard_map/all_to_all | solution.py:88
  15.6 2.3 copy-start.6
  31.6 31.8 %all-to-all-start = ((bf16[4,1,8,16,1024]{4,2,1,0,3:T(8,128)(2,1)}), bf16[4,1,8,16,1024]{4,2,1,0,3:T(8,128)(2,1)S(1)}, u32[]{:S(2)}, u32[]{:S(2)}) async-start(bf16[4,1,8,16,1024]{4,2,1,0,3:T(8,128)(2,1)} %pad_maximum_fusion.1), calls=%async_computation | async-start | bytes 2097152 | tf_op jit(solution)/shard_map/all_to_all | solution.py:87
  46.0 3.1 copy-start.12
  46.3 2.8 copy-start.9
  49.1 1.2 copy-start.10
  63.3 1.0 copy-start.4
  64.4 27.7 %all-to-all-start.3 = ((bf16[4,1,1,128,1024]{4,0,2,1,3:T(4,128)(2,1)}), bf16[4,1,1,128,1024]{4,0,2,1,3:T(4,128)(2,1)S(1)}, u32[]{:S(2)}, u32[]{:S(2)}) async-start(bf16[4,1,1,128,1024]{4,0,2,1,3:T(4,128)(2,1)} %pad_maximum_fusion.4), calls=%async_computation.3 | async-start | bytes 2097152 | tf_op jit(solution)/shard_map/all_to_all | solution.py:100
  74.7 4.7 %copy-start.13 = (bf16[128,16,64]{0,2,1:T(8,128)(2,1)}, bf16[128,16,64]{0,2,1:T(8,128)(2,1)S(1)}, u32[]{:S(2)}) copy-start(bf16[128,16,64]{0,2,1:T(8,128)(2,1)S(1)} %copy.197) | copy-start | bytes 786436
  75.0 2.8 copy-start.11
  77.9 1.5 copy-start.8
  92.0 31.3 %all-to-all-start.1 = ((bf16[4,1,128,1,1024]{4,0,3,1,2:T(4,128)(2,1)}), bf16[4,1,128,1,1024]{4,0,3,1,2:T(4,128)(2,1)}, u32[]{:S(2)}, u32[]{:S(2)}) async-start(bf16[4,1,128,1,1024]{4,0,3,1,2:T(4,128)(2,1)} %pad_maximum_fusion.2), calls=%async_computation.1 | async-start | bytes 2097152 | tf_op jit(solution)/shard_map/all_to_all | solution.py:93
  100.0 147.7 %reduce-scatter.7.cloned.1.call-start = ((), (), s32[]{:S(2)}) async-start(), calls=%async_computation.6 | async-start | bytes 8912896
  124.9 1.0 copy-start.5
  125.0 2.4 copy-start.2
  140.6 186.7 %reduce-scatter.9.cloned.1.call-start = ((), (), s32[]{:S(2)}) async-start(), calls=%async_computation.7 | async-start | bytes 557056
  251.3 78.4 %copy-start.1 = (bf16[1024,1024]{1,0:T(8,128)(2,1)S(1)}, bf16[1024,1024]{1,0:T(8,128)(2,1)}, u32[]{:S(2)}) copy-start(bf16[1024,1024]{1,0:T(8,128)(2,1)} %param.9) | copy-start | bytes 6291460
Sparse Core Ops, SparseCore 0:
  140.8 106.8 reduce-scatter.6
  251.7 75.5 reduce-scatter.8
where the time goes:
time: 338 us; the launch traced here: 337 us
  waiting for transfers between devices  213 us (63%)
  local copies, waits for them, and re-layouts  48.6 us (14%)
  starting transfers between devices  25.2 us (7%)
  matrix products  20 us (6%)
  other arithmetic  15.3 us (5%)
  between operations  14.5 us (4%)
    unnamed x4, waiting for transfers between devices  179 us
    unnamed x40, local copies, waits for them, and re-layouts  24.6 us
    all_to_all x1, waiting for transfers between devices, local(): lax.all_to_all(jnp.concatenate([temporal_grads, temporal_out[None]], axis...  19.8 us
    all_to_all x1, waiting for transfers between devices, local(): lax.all_to_all(spatial_send, 'token', split_axis=2, concat_axis=3, tiled=...  12.1 us
    another operation x16, local copies, waits for them, and re-layouts  9.79 us
    all_to_all x1, starting transfers between devices, local(): lax.all_to_all(temporal_send, 'frame', split_axis=3, concat_axis=2, tiled...  8.99 us
    all_to_all x1, starting transfers between devices, local(): lax.all_to_all(jnp.concatenate([temporal_grads, temporal_out[None]], axis...  7.92 us
  transfers between devices with their start and end apart: 6, of which 5 were waited for; matrix products, arithmetic and copies ran while one was open for 17% of the time, Pallas kernels for 0%

commit v1 on v0

--- a/solution.py
+++ b/solution.py
@@ -78,54 +78,41 @@
     return (attn_out.reshape(grid_shape), stacked)
 
 
+def reduce_blocks(blocks, axis, dim):
+    parts = lax.axis_size(axis)
+    shape = blocks.shape
+    cut = blocks.reshape(shape[:dim] + (parts, shape[dim] // parts) + shape[dim + 1 :])
+    cut = jnp.moveaxis(cut, dim, 0)
+    landed = lax.all_to_all(cut.astype(jnp.bfloat16), axis, split_axis=0, concat_axis=0, tiled=True)
+    return jnp.sum(landed.astype(jnp.float32), axis=0)
+
+
+def outer(cotangent, branch_out):
+    width = cotangent.shape[-1]
+    return jnp.einsum(
+        "rd,re->de",
+        cotangent.reshape(-1, width),
+        branch_out.reshape(-1, width),
+        preferred_element_type=jnp.float32,
+    )
+
+
 def local(temporal_qkv, spatial_qkv, out_grad, temporal_proj, spatial_proj):
-    width = out_grad.shape[-1]
-    temporal_extra = project(out_grad, temporal_proj)
-    spatial_extra = project(out_grad, spatial_proj)
-    temporal_send = jnp.concatenate([temporal_qkv, temporal_extra[None]], axis=0)
-    spatial_send = jnp.concatenate([spatial_qkv, spatial_extra[None]], axis=0)
+    temporal_send = jnp.concatenate([temporal_qkv, out_grad[None]], axis=0)
+    spatial_send = jnp.concatenate([spatial_qkv, out_grad[None]], axis=0)
     temporal_recv = lax.all_to_all(temporal_send, "frame", split_axis=3, concat_axis=2, tiled=True)
     spatial_recv = lax.all_to_all(spatial_send, "token", split_axis=2, concat_axis=3, tiled=True)
-    temporal_branch = temporal_recv[3]
-    spatial_branch = spatial_recv[3]
+    temporal_branch = project(temporal_recv[3], temporal_proj)
+    spatial_branch = project(spatial_recv[3], spatial_proj)
     temporal_out, temporal_grads = attend(temporal_recv[:3], temporal_branch, True)
     spatial_out, spatial_grads = attend(spatial_recv[:3], spatial_branch, False)
-    temporal_back = lax.all_to_all(
-        jnp.concatenate([temporal_grads, temporal_out[None]], axis=0),
-        "frame",
-        split_axis=2,
-        concat_axis=3,
-        tiled=True,
-    )
-    spatial_back = lax.all_to_all(
-        jnp.concatenate([spatial_grads, spatial_out[None]], axis=0),
-        "token",
-        split_axis=3,
-        concat_axis=2,
-        tiled=True,
-    )
-    temporal_home = temporal_back[:3]
-    spatial_home = spatial_back[:3]
-    grad_pairs = ((out_grad, temporal_back[3]), (out_grad, spatial_back[3]))
-    flat_pairs = tuple(
-        (
-            (cotangent.reshape(-1, width), branch_out.reshape(-1, width))
-            for cotangent, branch_out in grad_pairs
-        )
-    )
-    row_share = width // lax.axis_size("frame")
-    blocks = []
-    for cotangent, branch_out in flat_pairs:
-        blocks.append(
-            jnp.einsum("rd,re->de", cotangent, branch_out, preferred_element_type=jnp.float32)
-        )
-    row_part = lax.psum_scatter(
-        jnp.concatenate(blocks, axis=1), "frame", scatter_dimension=0, tiled=True
-    )
-    summed = lax.psum_scatter(
-        row_part.reshape(row_share, 2, width), ("token", "dp"), scatter_dimension=2, tiled=True
-    )
-    return (temporal_home, spatial_home, summed[:, 0, :], summed[:, 1, :])
+    temporal_home = lax.all_to_all(temporal_grads, "frame", split_axis=2, concat_axis=3, tiled=True)
+    spatial_home = lax.all_to_all(spatial_grads, "token", split_axis=3, concat_axis=2, tiled=True)
+    blocks = jnp.stack([outer(temporal_recv[3], temporal_out), outer(spatial_recv[3], spatial_out)])
+    blocks = reduce_blocks(blocks, "token", 2)
+    blocks = reduce_blocks(blocks, "frame", 1)
+    blocks = reduce_blocks(blocks, "dp", 2)
+    return (temporal_home, spatial_home, blocks[0], blocks[1])
 
 
 def solution(mesh):

time: 338 us -> 229 us (0.68)
  waiting for transfers between devices: 213 us -> 93.4 us
  starting transfers between devices: 25.2 us -> 42.9 us
  between operations: 14.5 us -> 0.93 us
  matrix products: 20 us -> 26.4 us
  local copies, waits for them, and re-layouts: 48.6 us -> 44.5 us
    unnamed x4 -> x0, waiting for transfers between devices: 179 us -> none
    all_to_all x2 -> x5, waiting for transfers between devices: 19.8 us -> 68.9 us  [the longest x3 38.3 us: reduce_blocks(): lax.all_to_all(cut.astype(jnp.bfloat16), axis, split_axis=0, concat_axis=...]
    all_to_all x2 -> x5, starting transfers between devices: 11.7 us -> 29.6 us  [the longest x3 18.5 us: reduce_blocks(): lax.all_to_all(cut.astype(jnp.bfloat16), axis, split_axis=0, concat_axis=...]
    unnamed x40 -> x30, local copies, waits for them, and re-layouts: 24.6 us -> 7.01 us
    concatenate x5 -> x2, other arithmetic: 15.2 us -> 3.3 us  [the longest x1 2.22 us: local(): spatial_send = jnp.concatenate([spatial_qkv, out_grad[None]], axis=0)]
    all_to_all x1, waiting for transfers between devices: 1.58 us -> 11.2 us  [local(): lax.all_to_all(temporal_send, 'frame', split_axis=3, concat_axis=2, tiled...]
    another operation x0 -> x2, other arithmetic: none -> 7.97 us  [attend(): jnp.stack([query_grad, key_grad, value_grad]).reshape((3,) + grid_shape)]
    convert_element_type x0 -> x6, local copies, waits for them, and re-layouts: none -> 5.95 us  [the longest x4 4.27 us: reduce_blocks(): cut.astype(jnp.bfloat16)]
  transfers between devices with their start and end apart: 6 -> 7, of which waited for: 5 -> 6; matrix products, arithmetic and copies ran while one was open for 17% -> 25% of each run, Pallas kernels for 0% -> 0%
where the time goes in v1:
time: 229 us; the launch traced here: 225 us
  waiting for transfers between devices  93.4 us (41%)
  local copies, waits for them, and re-layouts  44.5 us (19%)
  starting transfers between devices  42.9 us (19%)
  matrix products  26.4 us (12%)
  other arithmetic  16.5 us (7%)
    all_to_all x3, waiting for transfers between devices, reduce_blocks(): lax.all_to_all(cut.astype(jnp.bfloat16), axis, split_axis=0, concat_axis=...  38.3 us
    all_to_all x1, waiting for transfers between devices, local(): lax.all_to_all(temporal_grads, 'frame', split_axis=2, concat_axis=3, tile...  20.4 us
    all_to_all x3, starting transfers between devices, reduce_blocks(): lax.all_to_all(cut.astype(jnp.bfloat16), axis, split_axis=0, concat_axis=...  18.5 us
    another operation x12, local copies, waits for them, and re-layouts  16.2 us
    all_to_all x1, waiting for transfers between devices, local(): lax.all_to_all(spatial_send, 'token', split_axis=2, concat_axis=3, tiled=...  13.3 us
    all_to_all x1, waiting for transfers between devices, local(): lax.all_to_all(temporal_send, 'frame', split_axis=3, concat_axis=2, tiled...  11.2 us
    all_to_all x1, waiting for transfers between devices, local(): lax.all_to_all(spatial_grads, 'token', split_axis=3, concat_axis=2, tiled...  10.3 us
    another operation x6, local copies, waits for them, and re-layouts, attend(): jnp.stack([query_grad, key_grad, value_grad]).reshape((3,) + grid_shape)  9.69 us
  transfers between devices with their start and end apart: 7, of which 6 were waited for; matrix products, arithmetic and copies ran while one was open for 25% of the time, Pallas kernels for 0%

profile of v1, /device:TPU:8, one launch (start us, length us, event | category | flops | bytes accessed | tf_op | source)
XLA Modules:
  0.0 224.6 jit_solution(17804478533072343454)
XLA Ops:
  0.6 1.2 copy.240
  2.1 2.2 pad_maximum_fusion.2
  4.3 4.3 %all-to-all-start.2 = ((bf16[4,1,8,16,1024]{4,3,1,0,2:T(8,128)(2,1)}), bf16[4,1,8,16,1024]{4,3,1,0,2:T(8,128)(2,1)S(1)}, u32[]{:S(2)}, u32[]{:S(2)}) async-start(bf16[4,1,8,16,1024]{4,3,1,0,2:T(8,128)(2,1)} %pad_maximum_fusion.2), calls=%async_computation.2 | async-start | bytes 2097152 | tf_op jit(solution)/shard_map/all_to_all | solution.py:104
  8.6 1.6 copy.154
  11.2 13.3 %all-to-all-done.2 = bf16[4,1,8,16,1024]{4,3,1,0,2:T(8,128)(2,1)S(1)} async-done(((bf16[4,1,8,16,1024]{4,3,1,0,2:T(8,128)(2,1)}), bf16[4,1,8,16,1024]{4,3,1,0,2:T(8,128)(2,1)S(1)}, u32[]{:S(2)}, u32[]{:S(2)}) %all-to-all-start.2) | async-done | bytes 1048608 | tf_op jit(solution)/shard_map/all_to_all | solution.py:104
  24.5 9.0 %all-to-all-start = ((bf16[4,1,8,16,1024]{4,2,0,1,3:T(8,128)(2,1)}), bf16[4,1,8,16,1024]{4,2,0,1,3:T(8,128)(2,1)}, u32[]{:S(2)}, u32[]{:S(2)}) async-start(bf16[4,1,8,16,1024]{4,2,0,1,3:T(8,128)(2,1)} %pad_maximum_fusion), calls=%async_computation | async-start | bytes 2097152 | tf_op jit(solution)/shard_map/all_to_all | solution.py:103
  34.4 1.3 reshape.227
  39.9 1.5 fusion.33
  41.3 1.7 fusion.14
  43.1 2.1 convert_bitcast_fusion
  45.2 11.2 %all-to-all-done = bf16[4,1,8,16,1024]{4,2,0,1,3:T(8,128)(2,1)} async-done(((bf16[4,1,8,16,1024]{4,2,0,1,3:T(8,128)(2,1)}), bf16[4,1,8,16,1024]{4,2,0,1,3:T(8,128)(2,1)}, u32[]{:S(2)}, u32[]{:S(2)}) %all-to-all-start) | async-done | bytes 1048608 | tf_op jit(solution)/shard_map/all_to_all | solution.py:103
  56.4 1.5 copy.238
  60.1 2.1 reshape.222
  62.2 2.2 copy.159
  64.4 2.1 reshape.220
  66.5 1.5 copy.156
  68.0 2.1 reshape.219
  70.1 2.2 copy.163
  72.2 2.5 %fusion.32 = (f32[16,128]{1,0:T(8,128)S(1)}, f32[16,128,128]{1,2,0:T(8,128)}) fusion(bf16[128,16,64]{0,2,1:T(8,128)(2,1)S(1)} %copy.156, bf16[128,16,64]{0,2,1:T(8,128)(2,1)} %copy.163), kind=kOutput, calls=%fused_computation.59 | convolution fusion | flops 34340992 | bytes 1581056 | tf_op jit(solution)/shard_map/sub | solution.py:35
  74.8 2.5 %fusion.15 = (f32[16,128]{1,0:T(8,128)S(1)}, bf16[16,64,128]{2,1,0:T(8,128)(2,1)}) fusion(bf16[128,1024]{0,1:T(8,128)(2,1)} %copy.158, bf16[128,16,64]{0,2,1:T(8,128)(2,1)} %copy.159, f32[16,128]{1,0:T(8,128)S(1)} %get-tuple-element.29, bf16[128,16,64]{0,2,1:T(8,128)(2,1)S(1)} %copy.156, bf16[128,16,64]{0,2,1:T(8,128)(2,1)} %copy.163), kind=kOutput, calls=%fused_computation.40 | convolution fusion | flops 68812928 | bytes 1327104 | tf_op jit(solution)/shard_map/cbhij,cjbhe->cibhe/dot_general | solution.py:37
  77.3 1.8 convert_bitcast_fusion.1
  79.5 2.3 %copy.193 = bf16[8,2,1024,128]{3,2,1,0:T(8,128)(2,1)} copy(bf16[8,2,1024,128]{3,2,0,1:T(8,128)(2,1)S(1)} %maximum_bitcast_fusion) | data formatting | bytes 8388608 | tf_op jit(solution)/shard_map/convert_element_type | solution.py:86
  81.8 4.9 %all-to-all-start.4 = ((bf16[8,2,1024,128]{3,2,1,0:T(8,128)(2,1)}), bf16[8,2,1024,128]{3,2,1,0:T(8,128)(2,1)}, u32[]{:S(2)}, u32[]{:S(2)}) async-start(bf16[8,2,1024,128]{3,2,1,0:T(8,128)(2,1)} %copy.193), calls=%async_computation.4 | async-start | bytes 8388608 | tf_op jit(solution)/shard_map/all_to_all | solution.py:86
  86.7 1.5 convolution_convert_fusion
  88.2 1.3 copy.189
  89.5 1.8 fusion.9
  92.5 1.3 copy.188
  93.8 2.1 fusion.12
  95.9 2.0 copy.187
  97.9 3.8 %pad_maximum_fusion.3 = bf16[3,1,1,128,1024]{4,0,2,1,3:T(4,128)(2,1)} fusion(bf16[1,1,1,128,1024]{4,0,2,1,3:T(2,128)(2,1)S(1)} %copy.189, bf16[1,1,1,128,1024]{4,0,2,1,3:T(2,128)(2,1)S(1)} %copy.188, bf16[1,1,1,128,1024]{4,0,2,1,3:T(2,128)(2,1)} %copy.187), kind=kLoop, calls=%fused_computation.34 | loop fusion | flops 2359296 | bytes 1572864 | tf_op jit(solution)/shard_map/stack | solution.py:77
  101.7 34.4 %all-to-all-done.4 = bf16[8,2,1024,128]{3,2,1,0:T(8,128)(2,1)} async-done(((bf16[8,2,1024,128]{3,2,1,0:T(8,128)(2,1)}), bf16[8,2,1024,128]{3,2,1,0:T(8,128)(2,1)}, u32[]{:S(2)}, u32[]{:S(2)}) %all-to-all-start.4) | async-done | bytes 4194336 | tf_op jit(solution)/shard_map/all_to_all | solution.py:86
  136.2 3.6 %all-to-all-start.3 = ((bf16[3,1,1,128,1024]{4,0,2,1,3:T(4,128)(2,1)}), bf16[3,1,1,128,1024]{4,0,2,1,3:T(4,128)(2,1)S(1)}, u32[]{:S(2)}, u32[]{:S(2)}) async-start(bf16[3,1,1,128,1024]{4,0,2,1,3:T(4,128)(2,1)} %pad_maximum_fusion.3), calls=%async_computation.3 | async-start | bytes 2097152 | tf_op jit(solution)/shard_map/all_to_all | solution.py:110
  139.7 3.7 %reduce_sum.53 = bf16[2,1024,128]{2,1,0:T(8,128)(2,1)} reduce(bf16[8,2,1024,128]{3,2,1,0:T(8,128)(2,1)} %all-to-all-done.4, bf16[]{:T(256)} %constant.3.clone.1), dimensions={0}, to_apply=%region_4.0 | reduce | flops 1835008 | bytes 4718594 | tf_op jit(solution)/shard_map/reduce_sum | solution.py:87
  143.4 1.9 copy.194
  145.3 10.3 %all-to-all-done.3 = bf16[3,1,1,128,1024]{4,0,2,1,3:T(4,128)(2,1)S(1)} async-done(((bf16[3,1,1,128,1024]{4,0,2,1,3:T(4,128)(2,1)}), bf16[3,1,1,128,1024]{4,0,2,1,3:T(4,128)(2,1)S(1)}, u32[]{:S(2)}, u32[]{:S(2)}) %all-to-all-start.3) | async-done | bytes 786464 | tf_op jit(solution)/shard_map/all_to_all | solution.py:110
  155.6 7.9 %all-to-all-start.5 = ((bf16[16,2,64,128]{3,2,1,0:T(8,128)(2,1)}), bf16[16,2,64,128]{3,2,1,0:T(8,128)(2,1)}, u32[]{:S(2)}, u32[]{:S(2)}) async-start(bf16[16,2,64,128]{3,2,1,0:T(8,128)(2,1)} %copy.194), calls=%async_computation.5 | async-start | bytes 1048576 | tf_op jit(solution)/shard_map/all_to_all | solution.py:86
  163.5 2.5 %convolution_convert_fusion.3 = bf16[16,64,128]{2,1,0:T(8,128)(2,1)} fusion(bf16[128,16,64]{0,2,1:T(8,128)(2,1)} %bitcast.189, f32[16,128]{1,0:T(8,128)S(1)} %get-tuple-element.29, bf16[128,16,64]{0,2,1:T(8,128)(2,1)S(1)} %copy.156, bf16[128,16,64]{0,2,1:T(8,128)(2,1)} %copy.163), kind=kOutput, calls=%fused_computation.28 | convolution fusion | flops 68290688 | bytes 1056768 | tf_op jit(solution)/shard_map/cbhij,cibhe->cjbhe/dot_general | solution.py:71
  166.0 2.0 copy.170
  168.0 1.8 fusion.8
  171.7 2.0 copy.169
  173.7 1.4 fusion.10
  176.2 4.1 %pad_maximum_fusion.1 = bf16[3,1,128,1,1024]{4,0,3,1,2:T(4,128)(2,1)} fusion(bf16[1,1,128,1,1024]{4,0,3,1,2:T(2,128)(2,1)} %copy.170, bf16[1,1,128,1,1024]{4,0,3,1,2:T(2,128)(2,1)} %copy.169, bf16[1,1,128,1,1024]{4,0,3,1,2:T(2,128)(2,1)} %copy.168), kind=kLoop, calls=%fused_computation.32 | loop fusion | flops 2359296 | bytes 1572864 | tf_op jit(solution)/shard_map/stack | solution.py:77
  180.4 7.5 %all-to-all-start.1 = ((bf16[3,1,128,1,1024]{4,0,3,1,2:T(4,128)(2,1)}), bf16[3,1,128,1,1024]{4,0,3,1,2:T(4,128)(2,1)}, u32[]{:S(2)}, u32[]{:S(2)}) async-start(bf16[3,1,128,1,1024]{4,0,3,1,2:T(4,128)(2,1)} %pad_maximum_fusion.1), calls=%async_computation.1 | async-start | bytes 2097152 | tf_op jit(solution)/shard_map/all_to_all | solution.py:109
  189.8 20.4 %all-to-all-done.1 = bf16[3,1,128,1,1024]{4,0,3,1,2:T(4,128)(2,1)} async-done(((bf16[3,1,128,1,1024]{4,0,3,1,2:T(4,128)(2,1)}), bf16[3,1,128,1,1024]{4,0,3,1,2:T(4,128)(2,1)}, u32[]{:S(2)}, u32[]{:S(2)}) %all-to-all-start.1) | async-done | bytes 786464 | tf_op jit(solution)/shard_map/all_to_all | solution.py:109
  210.2 5.8 %all-to-all-start.6 = ((bf16[2,2,4096]{2,1,0:T(2,128)(2,1)}), bf16[2,2,4096]{2,1,0:T(2,128)(2,1)S(1)}, u32[]{:S(2)}, u32[]{:S(2)}) async-start(bf16[2,2,4096]{2,1,0:T(2,128)(2,1)} %reshape.237), calls=%async_computation.6 | async-start | bytes 65536 | tf_op jit(solution)/shard_map/all_to_all | solution.py:86
  217.2 1.5 copy.239
  218.7 1.3 copy.196
  220.0 3.8 %all-to-all-done.6 = bf16[2,2,4096]{2,1,0:T(2,128)(2,1)S(1)} async-done(((bf16[2,2,4096]{2,1,0:T(2,128)(2,1)}), bf16[2,2,4096]{2,1,0:T(2,128)(2,1)S(1)}, u32[]{:S(2)}, u32[]{:S(2)}) %all-to-all-start.6) | async-done | bytes 32800 | tf_op jit(solution)/shard_map/all_to_all | solution.py:86
  (50 shorter events, 16.9 us)
Async XLA Ops:
  0.6 36.3 %copy-start = (bf16[1024,1024]{1,0:T(8,128)(2,1)S(1)}, bf16[1024,1024]{1,0:T(8,128)(2,1)}, u32[]{:S(2)}) copy-start(bf16[1024,1024]{1,0:T(8,128)(2,1)} %param.9) | copy-start | bytes 6291460
  4.3 20.3 %all-to-all-start.2 = ((bf16[4,1,8,16,1024]{4,3,1,0,2:T(8,128)(2,1)}), bf16[4,1,8,16,1024]{4,3,1,0,2:T(8,128)(2,1)S(1)}, u32[]{:S(2)}, u32[]{:S(2)}) async-start(bf16[4,1,8,16,1024]{4,3,1,0,2:T(8,128)(2,1)} %pad_maximum_fusion.2), calls=%async_computation.2 | async-start | bytes 2097152 | tf_op jit(solution)/shard_map/all_to_all | solution.py:104
  24.5 31.9 %all-to-all-start = ((bf16[4,1,8,16,1024]{4,2,0,1,3:T(8,128)(2,1)}), bf16[4,1,8,16,1024]{4,2,0,1,3:T(8,128)(2,1)}, u32[]{:S(2)}, u32[]{:S(2)}) async-start(bf16[4,1,8,16,1024]{4,2,0,1,3:T(8,128)(2,1)} %pad_maximum_fusion), calls=%async_computation | async-start | bytes 2097152 | tf_op jit(solution)/shard_map/all_to_all | solution.py:103
  35.8 2.4 %copy-start.10 = (bf16[1,1,8,16,1024]{4,3,1,0,2:T(8,128)(2,1)S(1)}, bf16[1,1,8,16,1024]{4,3,1,0,2:T(8,128)(2,1)}, u32[]{:S(2)}) copy-start(bf16[1,1,8,16,1024]{4,3,1,0,2:T(8,128)(2,1)} %get-tuple-element.22) | copy-start | bytes 786436
  36.9 2.1 copy-start.9
  39.0 4.1 %copy-start.5 = (bf16[128,16,64]{0,2,1:T(8,128)(2,1)}, bf16[128,16,64]{0,2,1:T(8,128)(2,1)S(1)}, u32[]{:S(2)}) copy-start(bf16[128,16,64]{0,2,1:T(8,128)(2,1)S(1)} %copy.174) | copy-start | bytes 786436
  39.9 3.3 %copy-start.7 = (bf16[128,16,64]{0,2,1:T(8,128)(2,1)}, bf16[128,16,64]{0,2,1:T(8,128)(2,1)S(1)}, u32[]{:S(2)}) copy-start(bf16[128,16,64]{0,2,1:T(8,128)(2,1)S(1)} %copy.182) | copy-start | bytes 786436
  56.4 2.4 %copy-start.2 = (bf16[1024,1024]{1,0:T(8,128)(2,1)S(1)}, bf16[1024,1024]{1,0:T(8,128)(2,1)}, u32[]{:S(2)}) copy-start(bf16[1024,1024]{1,0:T(8,128)(2,1)} %param.8) | copy-start | bytes 6291460
  77.3 1.8 copy-start.1
  81.8 4.9 %copy-start.6 = (bf16[128,16,64]{0,2,1:T(8,128)(2,1)S(1)}, bf16[128,16,64]{0,2,1:T(8,128)(2,1)}, u32[]{:S(2)}) copy-start(bf16[128,16,64]{0,2,1:T(8,128)(2,1)} %copy-done.5) | copy-start | bytes 786436
  81.8 4.9 %copy-start.8 = (bf16[128,16,64]{0,2,1:T(8,128)(2,1)S(1)}, bf16[128,16,64]{0,2,1:T(8,128)(2,1)}, u32[]{:S(2)}) copy-start(bf16[128,16,64]{0,2,1:T(8,128)(2,1)} %copy-done.7) | copy-start | bytes 786436
  81.8 4.9 %copy-start.11 = (bf16[128,1024]{0,1:T(8,128)(2,1)S(1)}, bf16[128,1024]{0,1:T(8,128)(2,1)}, u32[]{:S(2)}) copy-start(bf16[128,1024]{0,1:T(8,128)(2,1)} %copy.177) | copy-start | bytes 786436
  81.8 54.4 %all-to-all-start.4 = ((bf16[8,2,1024,128]{3,2,1,0:T(8,128)(2,1)}), bf16[8,2,1024,128]{3,2,1,0:T(8,128)(2,1)}, u32[]{:S(2)}, u32[]{:S(2)}) async-start(bf16[8,2,1024,128]{3,2,1,0:T(8,128)(2,1)} %copy.193), calls=%async_computation.4 | async-start | bytes 8388608 | tf_op jit(solution)/shard_map/all_to_all | solution.py:86
  91.3 1.2 copy-start.3
  136.2 19.4 %all-to-all-start.3 = ((bf16[3,1,1,128,1024]{4,0,2,1,3:T(4,128)(2,1)}), bf16[3,1,1,128,1024]{4,0,2,1,3:T(4,128)(2,1)S(1)}, u32[]{:S(2)}, u32[]{:S(2)}) async-start(bf16[3,1,1,128,1024]{4,0,2,1,3:T(4,128)(2,1)} %pad_maximum_fusion.3), calls=%async_computation.3 | async-start | bytes 2097152 | tf_op jit(solution)/shard_map/all_to_all | solution.py:110
  155.6 24.7 %all-to-all-start.5 = ((bf16[16,2,64,128]{3,2,1,0:T(8,128)(2,1)}), bf16[16,2,64,128]{3,2,1,0:T(8,128)(2,1)}, u32[]{:S(2)}, u32[]{:S(2)}) async-start(bf16[16,2,64,128]{3,2,1,0:T(8,128)(2,1)} %copy.194), calls=%async_computation.5 | async-start | bytes 1048576 | tf_op jit(solution)/shard_map/all_to_all | solution.py:86
  169.7 0.8 copy-start.4
  180.4 29.9 %all-to-all-start.1 = ((bf16[3,1,128,1,1024]{4,0,3,1,2:T(4,128)(2,1)}), bf16[3,1,128,1,1024]{4,0,3,1,2:T(4,128)(2,1)}, u32[]{:S(2)}, u32[]{:S(2)}) async-start(bf16[3,1,128,1,1024]{4,0,3,1,2:T(4,128)(2,1)} %pad_maximum_fusion.1), calls=%async_computation.1 | async-start | bytes 2097152 | tf_op jit(solution)/shard_map/all_to_all | solution.py:109
  210.2 13.6 %all-to-all-start.6 = ((bf16[2,2,4096]{2,1,0:T(2,128)(2,1)}), bf16[2,2,4096]{2,1,0:T(2,128)(2,1)S(1)}, u32[]{:S(2)}, u32[]{:S(2)}) async-start(bf16[2,2,4096]{2,1,0:T(2,128)(2,1)} %reshape.237), calls=%async_computation.6 | async-start | bytes 65536 | tf_op jit(solution)/shard_map/all_to_all | solution.py:86

commit v2 on v1

v2 whole, which is shorter than its diff:
```python
import jax
import jax.numpy as jnp
from jax import lax
from jax.experimental import pallas as pl
from jax.experimental.pallas import tpu as pltpu
from jax.sharding import PartitionSpec as P

MESH = pl.DeviceIdType.MESH
BF16 = jnp.bfloat16
F32 = jnp.float32
ROOT = 0.125
CHUNKS = 2
PAIRS = 4


def rows_dot(left, right):
    return lax.dot_general(left, right, (((0,), (0,)), ((), ())), preferred_element_type=F32)


def cols_dot(left, right):
    return lax.dot_general(left, right, (((1,), (1,)), ((), ())), preferred_element_type=F32)


def dot(left, right):
    return jnp.dot(left, right, preferred_element_type=F32)


def attend_pair(q, k, v, g):
    lane = lax.broadcasted_iota(jnp.int32, (128, 128), 1)
    low = lane < 64
    low_b = low.astype(F32).astype(BF16)
    high_b = (lane >= 64).astype(F32).astype(BF16)
    q2 = jnp.concatenate([q * low_b, q * high_b], axis=0)
    g2 = jnp.concatenate([g * low_b, g * high_b], axis=0)
    scores = cols_dot(q2, k)
    top = jnp.max(scores, axis=1, keepdims=True)
    grown = jnp.exp((scores - top) * ROOT)
    probs = grown * (1.0 / jnp.sum(grown, axis=1, keepdims=True))
    probs_low = probs.astype(BF16)
    out2 = dot(probs_low, v)
    out = jnp.where(low, out2[:128], out2[128:]).astype(BF16)
    prob_grad = cols_dot(g2, v)
    out_f = out.astype(F32)
    delta = jnp.sum(g2.astype(F32) * jnp.concatenate([out_f, out_f], axis=0), axis=1, keepdims=True)
    score_grad = (probs * (prob_grad - delta)).astype(BF16)
    dq2 = dot(score_grad, k)
    dq = jnp.where(low, dq2[:128], dq2[128:]) * ROOT
    dk = rows_dot(score_grad, q2) * ROOT
    dv = rows_dot(probs_low, g2)
    return out, dq, dk, dv


def shuffle_matrix():
    row = lax.broadcasted_iota(jnp.int32, (128, 128), 0)
    col = lax.broadcasted_iota(jnp.int32, (128, 128), 1)
    hit = ((row >> 3) == (col & 15)) & ((row & 7) == (col >> 4))
    return hit.astype(F32).astype(BF16)


def body(
    tqkv_hbm, squkv_hbm, grad_hbm, tproj_hbm, sproj_hbm,
    tout_hbm, sout_hbm, tproj_out, sproj_out,
    tqkv, grad, tproj, sproj,
    tg_send, tg_recv, tc_send, tc_recv, tg, tbranch, tchunk, tgrad, tb_send, tb_recv, tout, tattn,
    sg, sq, sbranch, sgrad, sattn,
    tg_peer, tattn_peer, sg_peer, sattn_peer,
    tpart, tx_a, tx_b, tx_c, tx_sum, ty_send, ty_recv, tz_send, tz_recv,
    spart, sy_a, sy_b, sy_c, sy_sum, sx_send, sx_recv, sz_send, sz_recv,
    load_sem, tg_ss, tg_rs, tc_ss, tc_rs, tb_ss, tb_rs,
    sg_ss, sg_rs, sq_ss, sq_rs, sb_ss, sb_rs, own_sem,
    pg_ss, pg_rs, po_ss, po_rs, ring_ss, ring_rs, y_ss, y_rs, x_ss, x_rs, tz_ss, tz_rs, sz_ss, sz_rs, out_sem,
):
    frame = lax.axis_index("frame")
    token = lax.axis_index("token")
    dp = lax.axis_index("dp")
    z, y = frame // 4, lax.rem(frame, 4)
    x, core = token // 2, lax.rem(token, 2)
    zslot = dp * 4 + z

    def frame_peer(d):
        return lax.rem(frame + d, 16)

    def token_peer(d):
        return lax.rem(token + d, 8)

    def x_peer(d):
        return lax.rem(x + d, 4) * 2 + core

    def y_peer(d):
        return z * 4 + lax.rem(y + d, 4)

    def z_peer(d):
        slot = lax.rem(zslot + d, 8)
        return slot // 4, lax.rem(slot, 4)

    def remote(src, dst, send_sem, recv_sem, device):
        return pltpu.make_async_remote_copy(
            src_ref=src, dst_ref=dst, send_sem=send_sem, recv_sem=recv_sem, device_id=device, device_id_type=MESH
        )

    loads = [
        pltpu.make_async_copy(grad_hbm, grad, load_sem.at[0]),
        pltpu.make_async_copy(tqkv_hbm, tqkv, load_sem.at[1]),
        pltpu.make_async_copy(tproj_hbm, tproj, load_sem.at[2]),
        pltpu.make_async_copy(sproj_hbm, sproj, load_sem.at[3]),
    ]
    for load in loads:
        load.start()

    barrier = pltpu.get_barrier_semaphore()

    def greet_frame(d, carry):
        pl.semaphore_signal(barrier, inc=1, device_id={"frame": frame_peer(d)}, device_id_type=MESH)
        return carry

    def greet_token(d, carry):
        pl.semaphore_signal(barrier, inc=1, device_id={"token": token_peer(d)}, device_id_type=MESH)
        return carry

    def greet_dp(d, carry):
        pl.semaphore_signal(
            barrier, inc=1, device_id={"dp": 1 - dp, "frame": lax.rem(z + d, 4) * 4 + y}, device_id_type=MESH
        )
        return carry

    lax.fori_loop(1, 16, greet_frame, 0)
    lax.fori_loop(1, 8, greet_token, 0)
    lax.fori_loop(0, 4, greet_dp, 0)

    shuffle = shuffle_matrix()
    loads[0].wait()
    halves = []
    for half in range(2):
        rows = dot(shuffle, grad[:, :, half * 512 : half * 512 + 512].reshape(128, 512))
        halves.append(rows.reshape(16, 8, 512))
    tg_send[...] = jnp.concatenate(halves, axis=1).astype(BF16)

    pl.semaphore_wait(barrier, 26)

    def tg_copy(d):
        peer = frame_peer(d)
        return remote(tg_send.at[peer], tg_recv.at[frame], tg_ss.at[d], tg_rs.at[d], {"frame": peer})

    def tc_copy(chunk, d):
        peer = frame_peer(d)
        return remote(
            tc_send.at[chunk, peer], tc_recv.at[chunk, frame], tc_ss.at[chunk, d], tc_rs.at[chunk, d], {"frame": peer}
        )

    def tb_copy(chunk, d):
        peer = frame_peer(d)
        return remote(
            tb_send.at[chunk, peer], tb_recv.at[chunk, frame], tb_ss.at[chunk, d], tb_rs.at[chunk, d], {"frame": peer}
        )

    def token_rows(who):
        return pl.ds(pl.multiple_of(who * 16, 16), 16)

    def sg_copy(d):
        peer = token_peer(d)
        return remote(grad_hbm.at[peer], sg.at[token_rows(token)], sg_ss.at[d], sg_rs.at[d], {"token": peer})

    def sq_copy(d):
        peer = token_peer(d)
        return remote(squkv_hbm.at[:, peer], sq.at[:, token_rows(token)], sq_ss.at[d], sq_rs.at[d], {"token": peer})

    def sb_copy(d):
        peer = token_peer(d)
        return remote(sgrad.at[:, token_rows(peer)], sout_hbm.at[:, token], sb_ss.at[d], sb_rs.at[d], {"token": peer})

    def each(low, high, make, act):
        def step(d, carry):
            act(make(d))
            return carry

        lax.fori_loop(low, high, step, 0)

    def start(copy):
        copy.start()

    def arrive(copy):
        copy.wait_recv()

    def leave(copy):
        copy.wait_send()

    each(1, 16, tg_copy, start)
    each(1, 8, sg_copy, start)
    own_g = pltpu.make_async_copy(grad_hbm.at[token], sg.at[token_rows(token)], own_sem.at[0])
    own_q = pltpu.make_async_copy(squkv_hbm.at[:, token], sq.at[:, token_rows(token)], own_sem.at[1])
    own_g.start()
    own_q.start()
    each(1, 8, sq_copy, start)

    loads[1].wait()
    for chunk in range(CHUNKS):
        for a in range(3):
            pieces = []
            for i in range(PAIRS):
                at = (2 * i + chunk) * 128
                rows = dot(shuffle, tqkv[a, :, :, at : at + 128].reshape(128, 128))
                pieces.append(rows.reshape(16, 8, 128))
            first = jnp.concatenate(pieces[:2], axis=2)
            second = jnp.concatenate(pieces[2:], axis=2)
            tc_send[chunk, :, a * 16 : a * 16 + 16, :] = jnp.concatenate([first, second], axis=1).astype(BF16)
        each(1, 16, lambda d: tc_copy(chunk, d), start)
        tc_recv[chunk, frame] = tc_send[chunk, frame]
    tg_recv[frame] = tg_send[frame]

    peer_core = {"token": token + 1 - 2 * core}
    each(1, 16, tg_copy, arrive)
    loads[2].wait()
    landed = tg_recv[...].astype(F32).reshape(16, 2, 8, 512)
    for half in range(2):
        tg[:, half * 512 : half * 512 + 512] = landed[:, half].reshape(128, 512).astype(BF16)
    tg_pair = remote(tg, tg_peer, pg_ss.at[0], pg_rs.at[0], peer_core)
    tg_pair.start()
    for col in range(0, 1024, 256):
        tbranch[:, col : col + 256] = dot(tg[...], tproj[:, col : col + 256]).astype(BF16)

    own_g.wait()
    each(1, 8, sg_copy, arrive)
    loads[3].wait()
    sg_pair = remote(sg, sg_peer, pg_ss.at[1], pg_rs.at[1], peer_core)
    sg_pair.start()
    for col in range(0, 1024, 256):
        sbranch[:, col : col + 256] = dot(sg[...], sproj[:, col : col + 256]).astype(BF16)

    def temporal_chunk(chunk):
        each(1, 16, lambda d: tc_copy(chunk, d), arrive)
        for a in range(3):
            block = tc_recv[chunk, :, a * 16 : a * 16 + 16, :].astype(F32).reshape(16, 2, 8, 256)
            for half in range(2):
                tchunk[a, :, half * 256 : half * 256 + 256] = block[:, half].reshape(128, 256).astype(BF16)

        def pair(i, carry):
            here = pl.ds(pl.multiple_of(i * 128, 128), 128)
            there = pl.ds(pl.multiple_of((2 * i + chunk) * 128, 128), 128)
            out, dq, dk, dv = attend_pair(tchunk[0, :, here], tchunk[1, :, here], tchunk[2, :, here], tbranch[:, there])
            tattn[chunk, :, here] = out
            tgrad[0, :, here] = dq
            tgrad[1, :, here] = dk
            tgrad[2, :, here] = dv
            return carry

        lax.fori_loop(0, PAIRS, pair, 0)
        for a in range(3):
            rows = tgrad[a].reshape(16, 8, 512)
            tb_send[chunk, :, a * 16 : a * 16 + 16, :] = jnp.concatenate(
                [rows[:, :, :256], rows[:, :, 256:]], axis=1
            ).astype(BF16)
        each(1, 16, lambda d: tb_copy(chunk, d), start)
        tb_recv[chunk, frame] = tb_send[chunk, frame]

    tattn_pair = remote(tattn.at[1 - core], tattn_peer, po_ss.at[0], po_rs.at[0], peer_core)
    sattn_pair = remote(sattn.at[1 - core], sattn_peer, po_ss.at[1], po_rs.at[1], peer_core)

    left_x, right_x = {"token": x_peer(3)}, {"token": x_peer(1)}
    left_y, right_y = {"frame": y_peer(3)}, {"frame": y_peer(1)}
    tx_copies = [
        remote(tpart.at[lax.rem(x + 2, 4)], tx_a, ring_ss.at[0], ring_rs.at[0], left_x),
        remote(tpart.at[lax.rem(x + 1, 4)], tx_b, ring_ss.at[1], ring_rs.at[1], right_x),
        remote(tx_sum, tx_c, ring_ss.at[2], ring_rs.at[2], left_x),
    ]
    sy_copies = [
        remote(spart.at[lax.rem(y + 2, 4)], sy_a, ring_ss.at[3], ring_rs.at[3], left_y),
        remote(spart.at[lax.rem(y + 1, 4)], sy_b, ring_ss.at[4], ring_rs.at[4], right_y),
        remote(sy_sum, sy_c, ring_ss.at[5], ring_rs.at[5], left_y),
    ]

    def temporal_partial(chunk):
        tg_pair.wait_recv()
        tattn_pair.wait_recv()
        rows_g = jnp.concatenate([tg[...], tg_peer[...]], axis=0)
        rows_o = jnp.concatenate([tattn[chunk], tattn_peer[...]], axis=0)
        for block in range(4):
            part = rows_dot(rows_g[:, block * 256 : block * 256 + 256], rows_o).astype(BF16)
            for i in range(4):
                tpart[i, block * 256 : block * 256 + 256, :] = part[:, i * 128 : i * 128 + 128]
        tx_copies[0].start()
        tx_copies[1].start()

    def temporal_relay():
        tx_copies[0].wait_recv()
        tx_sum[...] = (tpart[lax.rem(x + 3, 4)].astype(F32) + tx_a[...].astype(F32)).astype(BF16)
        tx_copies[2].start()

    temporal_chunk(0)

    @pl.when(core == 1)
    def _():
        tattn_pair.start()

    @pl.when(core == 0)
    def _():
        temporal_partial(0)

    own_q.wait()
    each(1, 8, sq_copy, arrive)

    def spatial_pair(i, carry):
        for c in range(2):
            at = pl.ds(pl.multiple_of((2 * i + c) * 128, 128), 128)
            here = pl.ds(pl.multiple_of(i * 128, 128), 128)
            out, dq, dk, dv = attend_pair(sq[0, :, at], sq[1, :, at], sq[2, :, at], sbranch[:, at])
            sattn[c, :, here] = out
            sgrad[0, :, at] = dq.astype(BF16)
            sgrad[1, :, at] = dk.astype(BF16)
            sgrad[2, :, at] = dv.astype(BF16)
        return carry

    lax.fori_loop(0, 4, spatial_pair, 0)
    sattn_pair.start()
    each(1, 8, sb_copy, start)
    own_b = pltpu.make_async_copy(sgrad.at[:, token_rows(token)], sout_hbm.at[:, token], own_sem.at[2])
    own_b.start()

    @pl.when(core == 0)
    def _():
        temporal_relay()

    sg_pair.wait_recv()
    sattn_pair.wait_recv()
    rows_g = jnp.concatenate([sg[...], sg_peer[...]], axis=0)
    rows_o = jnp.concatenate([sattn[core], sattn_peer[...]], axis=0)
    for block in range(4):
        part = rows_dot(rows_g[:, block * 256 : block * 256 + 256], rows_o).astype(BF16)
        for i in range(4):
            spart[i, block * 64 : block * 64 + 64, :] = part[i * 64 : i * 64 + 64]
    sy_copies[0].start()
    sy_copies[1].start()

    temporal_chunk(1)

    @pl.when(core == 0)
    def _():
        tattn_pair.start()

    @pl.when(core == 1)
    def _():
        temporal_partial(1)

    sy_copies[0].wait_recv()
    sy_sum[...] = (spart[lax.rem(y + 3, 4)].astype(F32) + sy_a[...].astype(F32)).astype(BF16)
    sy_copies[2].start()

    @pl.when(core == 1)
    def _():
        temporal_relay()

    def sx_copy(d):
        to = lax.rem(x + d, 4)
        return remote(sx_send.at[to], sx_recv.at[x], x_ss.at[d], x_rs.at[d], {"token": to * 2 + core})

    def ty_copy(d):
        to = lax.rem(y + d, 4)
        return remote(ty_send.at[to], ty_recv.at[y], y_ss.at[d], y_rs.at[d], {"frame": z * 4 + to})

    def z_copy(send, recv, ss, rs, d):
        to_dp, to_z = z_peer(d)
        return remote(send.at[to_z], recv.at[zslot], ss.at[d], rs.at[d], {"dp": to_dp, "frame": to_z * 4 + y})

    def tz_copy(d):
        return z_copy(tz_send, tz_recv, tz_ss, tz_rs, d)

    def sz_copy(d):
        return z_copy(sz_send, sz_recv, sz_ss, sz_rs, d)

    sy_copies[1].wait_recv()
    sy_copies[2].wait_recv()
    total = spart[y].astype(F32) + sy_b[...].astype(F32) + sy_c[...].astype(F32)
    for i in range(4):
        sx_send[i] = total[:, i * 128 : i * 128 + 128].astype(BF16)
    each(1, 4, sx_copy, start)

    tx_copies[1].wait_recv()
    tx_copies[2].wait_recv()
    total = tpart[x].astype(F32) + tx_b[...].astype(F32) + tx_c[...].astype(F32)
    for block in range(4):
        for i in range(4):
            at = block * 256 + i * 64
            ty_send[i, block * 64 : block * 64 + 64, :] = total[at : at + 64].astype(BF16)
    each(1, 4, ty_copy, start)

    sx_recv[x] = sx_send[x]
    each(1, 4, sx_copy, arrive)
    total = jnp.sum(sx_recv[...].astype(F32), axis=0).reshape(4, 64, 128)
    sz_send[...] = total.astype(BF16)
    each(1, 8, sz_copy, start)
    sz_recv[zslot] = sz_send[z]

    ty_recv[y] = ty_send[y]
    each(1, 4, ty_copy, arrive)
    total = jnp.sum(ty_recv[...].astype(F32), axis=0).reshape(4, 64, 128)
    tz_send[...] = total.astype(BF16)
    each(1, 8, tz_copy, start)
    tz_recv[zslot] = tz_send[z]

    for chunk in range(CHUNKS):
        each(1, 16, lambda d: tb_copy(chunk, d), arrive)
        for a in range(3):
            block = tb_recv[chunk, :, a * 16 : a * 16 + 16, :].astype(F32).reshape(16, 2, 8, 256)
            for half in range(2):
                rows = rows_dot(shuffle, block[:, half].reshape(128, 256).astype(BF16)).astype(BF16)
                for i in range(2):
                    at = (2 * (2 * half + i) + chunk) * 128
                    tout[a, :, :, at : at + 128] = rows[:, i * 128 : i * 128 + 128].reshape(8, 16, 128)
    store = pltpu.make_async_copy(tout, tout_hbm, out_sem)
    store.start()

    each(1, 8, sz_copy, arrive)
    total = jnp.sum(sz_recv[...].astype(F32), axis=0)
    sproj_out[...] = jnp.where(dp == 1, total[:, 64:], total[:, :64])
    each(1, 8, tz_copy, arrive)
    total = jnp.sum(tz_recv[...].astype(F32), axis=0)
    tproj_out[...] = jnp.where(dp == 1, total[:, 64:], total[:, :64])

    each(1, 8, sb_copy, arrive)
    each(1, 16, tg_copy, leave)
    for chunk in range(CHUNKS):
        each(1, 16, lambda d: tc_copy(chunk, d), leave)
        each(1, 16, lambda d: tb_copy(chunk, d), leave)
    each(1, 8, sg_copy, leave)
    each(1, 8, sq_copy, leave)
    each(1, 8, sb_copy, leave)
    each(1, 4, sx_copy, leave)
    each(1, 4, ty_copy, leave)
    each(1, 8, sz_copy, leave)
    each(1, 8, tz_copy, leave)
    for copy in [tg_pair, sg_pair, tattn_pair, sattn_pair] + tx_copies + sy_copies:
        copy.wait_send()
    own_b.wait()
    store.wait()


def local(temporal_qkv, spatial_qkv, out_grad, temporal_proj, spatial_proj):
    def vm(*shape):
        return pltpu.VMEM(shape, BF16)

    def dma(*shape):
        return pltpu.SemaphoreType.DMA(shape)

    any_spec = pl.BlockSpec(memory_space=pl.ANY)
    vmem_spec = pl.BlockSpec(memory_space=pltpu.VMEM)
    tout, sout, tproj, sproj = pl.pallas_call(
        body,
        out_shape=(
            jax.ShapeDtypeStruct((3, 8, 16, 1024), BF16),
            jax.ShapeDtypeStruct((3, 8, 16, 1024), BF16),
            jax.ShapeDtypeStruct((64, 64), F32),
            jax.ShapeDtypeStruct((64, 64), F32),
        ),
        in_specs=[any_spec] * 5,
        out_specs=(any_spec, any_spec, vmem_spec, vmem_spec),
        scratch_shapes=[
            vm(3, 8, 16, 1024), vm(8, 16, 1024), vm(1024, 1024), vm(1024, 1024),
            vm(16, 16, 512), vm(16, 16, 512), vm(2, 16, 48, 256), vm(2, 16, 48, 256),
            vm(128, 1024), vm(128, 1024), vm(3, 128, 512), pltpu.VMEM((3, 128, 512), F32),
            vm(2, 16, 48, 256), vm(2, 16, 48, 256), vm(3, 8, 16, 1024), vm(2, 128, 512),
            vm(128, 1024), vm(3, 128, 1024), vm(128, 1024), vm(3, 128, 1024), vm(2, 128, 512),
            vm(128, 1024), vm(128, 512), vm(128, 1024), vm(128, 512),
            vm(4, 1024, 128), vm(1024, 128), vm(1024, 128), vm(1024, 128), vm(1024, 128),
            vm(4, 256, 128), vm(4, 256, 128), vm(4, 64, 128), vm(8, 64, 128),
            vm(4, 256, 512), vm(256, 512), vm(256, 512), vm(256, 512), vm(256, 512),
            vm(4, 256, 128), vm(4, 256, 128), vm(4, 64, 128), vm(8, 64, 128),
            dma(4), dma(16), dma(16), dma(2, 16), dma(2, 16), dma(2, 16), dma(2, 16),
            dma(8), dma(8), dma(8), dma(8), dma(8), dma(8), dma(3),
            dma(2), dma(2), dma(2), dma(2), dma(6), dma(6), dma(4), dma(4), dma(4), dma(4),
            dma(8), dma(8), dma(8), dma(8), pltpu.SemaphoreType.DMA,
        ],
        compiler_params=pltpu.CompilerParams(
            collective_id=0, has_side_effects=True, vmem_limit_bytes=48 * 1024 * 1024
        ),
    )(
        temporal_qkv.reshape(3, 8, 16, 1024),
        spatial_qkv.reshape(3, 8, 16, 1024),
        out_grad.reshape(8, 16, 1024),
        temporal_proj,
        spatial_proj,
    )
    shape = (3, 1, 8, 16, 1024)
    return tout.reshape(shape), sout.reshape(shape), tproj, sproj


def solution(mesh):
    in_specs = (
        P(None, "dp", "frame", "token", None),
        P(None, "dp", "frame", "token", None),
        P("dp", "frame", "token", None),
        P(),
        P(),
    )
    out_specs = (
        P(None, "dp", "frame", "token", None),
        P(None, "dp", "frame", "token", None),
        P("frame", ("token", "dp")),
        P("frame", ("token", "dp")),
    )
    return jax.shard_map(local, mesh=mesh, in_specs=in_specs, out_specs=out_specs, check_vma=False)
```

time: 229 us -> 84.9 us (0.37); the launches traced: 225 us -> 84.7 us
  waiting for transfers between devices: 93.4 us -> 0 us
  Pallas kernels: 0 us -> 76.2 us
  starting transfers between devices: 42.9 us -> 0 us
  local copies, waits for them, and re-layouts: 44.5 us -> 7.79 us
  matrix products: 26.4 us -> 0 us
  other arithmetic: 16.5 us -> 0 us
    all_to_all x7 -> x0, waiting for transfers between devices: 93.4 us -> none  [the longest x3 38.3 us: reduce_blocks(): lax.all_to_all(cut.astype(jnp.bfloat16), axis, split_axis=0, concat_axis=...]
    pallas_call x0 -> x1, Pallas kernels: none -> 76.2 us  [local(): pl.pallas_call(body, out_shape=(jax.ShapeDtypeStruct((3, 8, 16, 1024), BF...]
    all_to_all x7 -> x0, starting transfers between devices: 42.9 us -> none  [the longest x3 18.5 us: reduce_blocks(): lax.all_to_all(cut.astype(jnp.bfloat16), axis, split_axis=0, concat_axis=...]
    another operation x18 -> x0, local copies, waits for them, and re-layouts: 25.9 us -> none
    dot_general x14 -> x0, matrix products: 22.4 us -> none  [the longest x2 4.27 us: attend(): jnp.einsum(pair_spec + ',' + col_spec + '->' + row_spec, probs_low, value...]
    another operation x2 -> x0, other arithmetic: 7.97 us -> none  [attend(): jnp.stack([query_grad, key_grad, value_grad]).reshape((3,) + grid_shape)]
    convert_element_type x6 -> x0, local copies, waits for them, and re-layouts: 5.95 us -> none  [the longest x4 4.27 us: reduce_blocks(): cut.astype(jnp.bfloat16)]
    reduce_sum x3 -> x0, other arithmetic: 4.84 us -> none  [reduce_blocks(): return jnp.sum(landed.astype(jnp.float32), axis=0)]
  transfers between devices with their start and end apart: 7 -> 0, of which waited for: 6 -> 0; matrix products, arithmetic and copies ran while one was open for 25% -> 0% of each run, Pallas kernels for 0% -> 0%
where the time goes in v2:
time: 84.9 us; the launch traced here: 84.7 us
  Pallas kernels  76.2 us (90%)
  local copies, waits for them, and re-layouts  7.79 us (9%)
    pallas_call x1, Pallas kernels, local(): pl.pallas_call(body, out_shape=(jax.ShapeDtypeStruct((3, 8, 16, 1024), BF...  76.2 us
    unnamed x12, local copies, waits for them, and re-layouts  7.79 us

profile of v2, /device:TPU:8, one launch (start us, length us, event | category | flops | bytes accessed | tf_op | source)
XLA Modules:
  0.0 84.7 jit_solution(7765170980394937392)
XLA Ops:
  0.6 0.0 copy-start
  0.6 1.6 %copy-done = bf16[1024,1024]{1,0:T(8,128)(2,1)S(1)} copy-done((bf16[1024,1024]{1,0:T(8,128)(2,1)S(1)}, bf16[1024,1024]{1,0:T(8,128)(2,1)}, u32[]{:S(2)}) %copy-start) | copy-done | bytes 2097176
  2.2 0.0 copy-start.1
  2.2 1.1 %copy-done.1 = bf16[3,1,8,16,1024]{4,3,2,1,0:T(8,128)(2,1)S(1)} copy-done((bf16[3,1,8,16,1024]{4,3,2,1,0:T(8,128)(2,1)S(1)}, bf16[3,1,8,16,1024]{4,3,2,1,0:T(8,128)(2,1)}, u32[]{:S(2)}) %copy-start.1) | copy-done | bytes 786456
  3.4 0.0 copy-start.2
  3.4 1.1 %copy-done.2 = bf16[3,1,8,16,1024]{4,3,2,1,0:T(8,128)(2,1)S(1)} copy-done((bf16[3,1,8,16,1024]{4,3,2,1,0:T(8,128)(2,1)S(1)}, bf16[3,1,8,16,1024]{4,3,2,1,0:T(8,128)(2,1)}, u32[]{:S(2)}) %copy-start.2) | copy-done | bytes 786456
  4.5 0.0 copy-start.3
  4.5 0.9 %copy-done.3 = bf16[1,8,16,1024]{3,2,1,0:T(8,128)(2,1)S(1)} copy-done((bf16[1,8,16,1024]{3,2,1,0:T(8,128)(2,1)S(1)}, bf16[1,8,16,1024]{3,2,1,0:T(8,128)(2,1)}, u32[]{:S(2)}) %copy-start.3) | copy-done | bytes 262168
  5.4 76.2 %shard_map.84 = (bf16[3,8,16,1024]{3,2,1,0:T(8,128)(2,1)S(1)}, bf16[3,8,16,1024]{3,2,1,0:T(8,128)(2,1)S(1)}, f32[64,64]{1,0:T(8,128)S(1)}, f32[64,64]{1,0:T(8,128)S(1)}) custom-call(bf16[3,8,16,1024]{3,2,1,0:T(8,128)(2,1)S(1)} %bitcast.11, bf16[3,8,16,1024]{3,2,1,0:T(8,128)(2,1)S(1)} %bitcast.12, bf16[8,16,1024]{2,1,0:T(8,128)(2,1)S(1)} %bitcast.13, ...), custom_call_target="tpu_custom_call" | custom-call | tf_op jit(solution)/shard_map/pallas_call | solution.py:445
  81.7 0.9 %copy.15 = bf16[3,1,8,16,1024]{4,3,2,1,0:T(8,128)(2,1)} copy(bf16[3,1,8,16,1024]{4,3,2,1,0:T(8,128)(2,1)S(1)} %bitcast.10) | data formatting | bytes 1572864
  82.6 0.9 %copy.16 = bf16[3,1,8,16,1024]{4,3,2,1,0:T(8,128)(2,1)} copy(bf16[3,1,8,16,1024]{4,3,2,1,0:T(8,128)(2,1)S(1)} %bitcast.9) | data formatting | bytes 1572864
  83.5 0.6 copy.17
  84.1 0.6 copy.18
Async XLA Ops:
  0.6 1.6 %copy-start = (bf16[1024,1024]{1,0:T(8,128)(2,1)S(1)}, bf16[1024,1024]{1,0:T(8,128)(2,1)}, u32[]{:S(2)}) copy-start(bf16[1024,1024]{1,0:T(8,128)(2,1)} %tproj_hbm.1) | copy-start | bytes 6291460
  2.2 1.1 %copy-start.1 = (bf16[3,1,8,16,1024]{4,3,2,1,0:T(8,128)(2,1)S(1)}, bf16[3,1,8,16,1024]{4,3,2,1,0:T(8,128)(2,1)}, u32[]{:S(2)}) copy-start(bf16[3,1,8,16,1024]{4,3,2,1,0:T(8,128)(2,1)} %param.5) | copy-start | bytes 2359300
  3.4 1.1 %copy-start.2 = (bf16[3,1,8,16,1024]{4,3,2,1,0:T(8,128)(2,1)S(1)}, bf16[3,1,8,16,1024]{4,3,2,1,0:T(8,128)(2,1)}, u32[]{:S(2)}) copy-start(bf16[3,1,8,16,1024]{4,3,2,1,0:T(8,128)(2,1)} %param.6) | copy-start | bytes 2359300
  4.5 0.9 %copy-start.3 = (bf16[1,8,16,1024]{3,2,1,0:T(8,128)(2,1)S(1)}, bf16[1,8,16,1024]{3,2,1,0:T(8,128)(2,1)}, u32[]{:S(2)}) copy-start(bf16[1,8,16,1024]{3,2,1,0:T(8,128)(2,1)} %param.7) | copy-start | bytes 786436

commit v3 on v2

v3 whole, which is shorter than its diff:
```python
import jax
import jax.numpy as jnp
from jax import lax
from jax.experimental import pallas as pl
from jax.experimental.pallas import tpu as pltpu
from jax.sharding import PartitionSpec as P

MESH = pl.DeviceIdType.MESH
BF16 = jnp.bfloat16
F32 = jnp.float32
ROOT = 0.125
CHUNKS = 2
PAIRS = 4


def rows_dot(left, right):
    return lax.dot_general(left, right, (((0,), (0,)), ((), ())), preferred_element_type=F32)


def cols_dot(left, right):
    return lax.dot_general(left, right, (((1,), (1,)), ((), ())), preferred_element_type=F32)


def dot(left, right):
    return jnp.dot(left, right, preferred_element_type=F32)


def attend_pair(q, k, v, g):
    lane = lax.broadcasted_iota(jnp.int32, (128, 128), 1)
    low = lane < 64
    low_b = low.astype(F32).astype(BF16)
    high_b = (lane >= 64).astype(F32).astype(BF16)
    q2 = jnp.concatenate([q * low_b, q * high_b], axis=0)
    g2 = jnp.concatenate([g * low_b, g * high_b], axis=0)
    scores = cols_dot(q2, k)
    top = jnp.max(scores, axis=1, keepdims=True)
    grown = jnp.exp((scores - top) * ROOT)
    probs = grown * (1.0 / jnp.sum(grown, axis=1, keepdims=True))
    probs_low = probs.astype(BF16)
    out2 = dot(probs_low, v)
    out = jnp.where(low, out2[:128], out2[128:]).astype(BF16)
    prob_grad = cols_dot(g2, v)
    out_f = out.astype(F32)
    delta = jnp.sum(g2.astype(F32) * jnp.concatenate([out_f, out_f], axis=0), axis=1, keepdims=True)
    score_grad = (probs * (prob_grad - delta)).astype(BF16)
    dq2 = dot(score_grad, k)
    dq = jnp.where(low, dq2[:128], dq2[128:]) * ROOT
    dk = rows_dot(score_grad, q2) * ROOT
    dv = rows_dot(probs_low, g2)
    return out, dq, dk, dv


def shuffle_matrix():
    row = lax.broadcasted_iota(jnp.int32, (128, 128), 0)
    col = lax.broadcasted_iota(jnp.int32, (128, 128), 1)
    hit = ((row >> 3) == (col & 15)) & ((row & 7) == (col >> 4))
    return hit.astype(F32).astype(BF16)


def body(
    tqkv_hbm, squkv_hbm, grad_hbm, tproj_hbm, sproj_hbm,
    tout_hbm, sout_hbm, tproj_out, sproj_out,
    tqkv, grad, tproj, sproj,
    tg_send, tg_recv, tc_send, tc_recv, tg_all, tbranch, tchunk, tgrad, tb_send, tb_recv, tout, tattn,
    sg, sq, sbranch, sgrad, sattn,
    tattn_all, sg_peer, sattn_peer,
    ty_send, ty_recv, tz_send, tz_recv,
    spart, sy_a, sy_b, sy_c, sy_sum, sx_send, sx_recv, sz_send, sz_recv,
    load_sem, tg_ss, tg_rs, tc_ss, tc_rs, tb_ss, tb_rs,
    sg_ss, sg_rs, sq_ss, sq_rs, sb_ss, sb_rs, own_sem,
    pair_ss, pair_rs, ta_ss, ta_rs, tf_ss, tf_rs, to_ss, to_rs, ring_ss, ring_rs, ty_ss, ty_rs, sx_ss, sx_rs, tz_ss, tz_rs, sz_ss, sz_rs, out_sem,
):
    frame = lax.axis_index("frame")
    token = lax.axis_index("token")
    dp = lax.axis_index("dp")
    z, y = frame // 4, lax.rem(frame, 4)
    x, core = token // 2, lax.rem(token, 2)
    zslot = dp * 4 + z

    def frame_peer(d):
        return lax.rem(frame + d, 16)

    def token_peer(d):
        return lax.rem(token + d, 8)

    def x_peer(d):
        return lax.rem(x + d, 4) * 2 + core

    def y_peer(d):
        return z * 4 + lax.rem(y + d, 4)

    def remote(src, dst, send_sem, recv_sem, device):
        return pltpu.make_async_remote_copy(
            src_ref=src, dst_ref=dst, send_sem=send_sem, recv_sem=recv_sem, device_id=device, device_id_type=MESH
        )

    loads = [
        pltpu.make_async_copy(grad_hbm, grad, load_sem.at[0]),
        pltpu.make_async_copy(tqkv_hbm, tqkv, load_sem.at[1]),
        pltpu.make_async_copy(tproj_hbm, tproj, load_sem.at[2]),
        pltpu.make_async_copy(sproj_hbm, sproj, load_sem.at[3]),
    ]
    for load in loads:
        load.start()

    barrier = pltpu.get_barrier_semaphore()

    def greet_frame(d, carry):
        pl.semaphore_signal(barrier, inc=1, device_id={"frame": frame_peer(d)}, device_id_type=MESH)
        return carry

    def greet_token(d, carry):
        pl.semaphore_signal(barrier, inc=1, device_id={"token": token_peer(d)}, device_id_type=MESH)
        return carry

    def greet_dp(d, carry):
        pl.semaphore_signal(
            barrier, inc=1, device_id={"dp": 1 - dp, "frame": lax.rem(z + d, 4) * 4 + y}, device_id_type=MESH
        )
        return carry

    lax.fori_loop(1, 16, greet_frame, 0)
    lax.fori_loop(1, 8, greet_token, 0)
    lax.fori_loop(0, 4, greet_dp, 0)

    shuffle = shuffle_matrix()
    loads[0].wait()
    halves = []
    for half in range(2):
        rows = dot(shuffle, grad[:, :, half * 512 : half * 512 + 512].reshape(128, 512))
        halves.append(rows.reshape(16, 8, 512))
    tg_send[...] = jnp.concatenate(halves, axis=1).astype(BF16)

    loads[1].wait()
    for chunk in range(CHUNKS):
        for a in range(3):
            pieces = []
            for i in range(PAIRS):
                at = (2 * i + chunk) * 128
                rows = dot(shuffle, tqkv[a, :, :, at : at + 128].reshape(128, 128))
                pieces.append(rows.reshape(16, 8, 128))
            first = jnp.concatenate(pieces[:2], axis=2)
            second = jnp.concatenate(pieces[2:], axis=2)
            tc_send[chunk, :, a * 16 : a * 16 + 16, :] = jnp.concatenate([first, second], axis=1).astype(BF16)
        tc_recv[chunk, frame] = tc_send[chunk, frame]
    tg_recv[frame] = tg_send[frame]

    pl.semaphore_wait(barrier, 26)

    def tg_copy(d):
        peer = frame_peer(d)
        return remote(tg_send.at[peer], tg_recv.at[frame], tg_ss.at[d], tg_rs.at[d], {"frame": peer})

    def tc_copy(chunk, d):
        peer = frame_peer(d)
        return remote(
            tc_send.at[chunk, peer], tc_recv.at[chunk, frame], tc_ss.at[chunk, d], tc_rs.at[chunk, d], {"frame": peer}
        )

    def tb_copy(chunk, d):
        peer = frame_peer(d)
        return remote(
            tb_send.at[chunk, peer], tb_recv.at[chunk, frame], tb_ss.at[chunk, d], tb_rs.at[chunk, d], {"frame": peer}
        )

    def token_rows(who):
        return pl.ds(pl.multiple_of(who * 16, 16), 16)

    def sg_copy(d):
        peer = token_peer(d)
        return remote(grad_hbm.at[peer], sg.at[token_rows(token)], sg_ss.at[d], sg_rs.at[d], {"token": peer})

    def sq_copy(d):
        peer = token_peer(d)
        return remote(squkv_hbm.at[:, peer], sq.at[:, token_rows(token)], sq_ss.at[d], sq_rs.at[d], {"token": peer})

    def sb_copy(d):
        peer = token_peer(d)
        return remote(sgrad.at[:, token_rows(peer)], sout_hbm.at[:, token], sb_ss.at[d], sb_rs.at[d], {"token": peer})

    def each(low, high, make, act):
        def step(d, carry):
            act(make(d))
            return carry

        lax.fori_loop(low, high, step, 0)

    def start(copy):
        copy.start()

    def arrive(copy):
        copy.wait_recv()

    def leave(copy):
        copy.wait_send()

    each(1, 16, tg_copy, start)
    each(1, 16, lambda d: tc_copy(0, d), start)
    each(1, 8, sg_copy, start)
    own_g = pltpu.make_async_copy(grad_hbm.at[token], sg.at[token_rows(token)], own_sem.at[0])
    own_q = pltpu.make_async_copy(squkv_hbm.at[:, token], sq.at[:, token_rows(token)], own_sem.at[1])
    own_g.start()
    own_q.start()
    each(1, 8, sq_copy, start)

    each(1, 16, lambda d: tc_copy(1, d), start)

    peer_core = {"token": token + 1 - 2 * core}
    each(1, 16, tg_copy, arrive)
    loads[2].wait()
    landed = tg_recv[...].astype(F32).reshape(16, 2, 8, 512)
    for half in range(2):
        tg_all[token, :, half * 512 : half * 512 + 512] = landed[:, half].reshape(128, 512).astype(BF16)

    def ta_copy(d):
        to = lax.rem(x + d, 4) * 2 + core
        return remote(tg_all.at[token], tg_all.at[token], ta_ss.at[d], ta_rs.at[d], {"token": to})

    def tf_copy(d):
        of = lax.rem(x + 4 - d, 4) * 2 + core
        return remote(tg_all.at[of], tg_all.at[of], tf_ss.at[d], tf_rs.at[d], peer_core)

    each(1, 4, ta_copy, start)
    tf_copy(0).start()
    for col in range(0, 1024, 256):
        tbranch[:, col : col + 256] = dot(tg_all[token], tproj[:, col : col + 256]).astype(BF16)

    own_g.wait()
    each(1, 8, sg_copy, arrive)
    loads[3].wait()
    sg_pair = remote(sg, sg_peer, pair_ss.at[0], pair_rs.at[0], peer_core)
    sg_pair.start()
    for col in range(0, 1024, 256):
        sbranch[:, col : col + 256] = dot(sg[...], sproj[:, col : col + 256]).astype(BF16)

    def to_copy(d):
        peer = token_peer(d)
        return remote(tattn.at[peer], tattn_all.at[token], to_ss.at[d], to_rs.at[d], {"token": peer})

    def temporal_chunk(chunk):
        each(1, 16, lambda d: tc_copy(chunk, d), arrive)
        for a in range(3):
            block = tc_recv[chunk, :, a * 16 : a * 16 + 16, :].astype(F32).reshape(16, 2, 8, 256)
            for half in range(2):
                tchunk[a, :, half * 256 : half * 256 + 256] = block[:, half].reshape(128, 256).astype(BF16)

        def pair(i, carry):
            here = pl.ds(pl.multiple_of(i * 128, 128), 128)
            there = pl.ds(pl.multiple_of((2 * i + chunk) * 128, 128), 128)
            out, dq, dk, dv = attend_pair(tchunk[0, :, here], tchunk[1, :, here], tchunk[2, :, here], tbranch[:, there])
            tattn[2 * i + chunk] = out
            tgrad[0, :, here] = dq
            tgrad[1, :, here] = dk
            tgrad[2, :, here] = dv
            return carry

        lax.fori_loop(0, PAIRS, pair, 0, unroll=True)
        if chunk == 1:
            each(1, 8, to_copy, start)
            tattn_all[token] = tattn[token]
        for a in range(3):
            rows = tgrad[a].reshape(16, 8, 512)
            tb_send[chunk, :, a * 16 : a * 16 + 16, :] = jnp.concatenate(
                [rows[:, :, :256], rows[:, :, 256:]], axis=1
            ).astype(BF16)
        each(1, 16, lambda d: tb_copy(chunk, d), start)
        tb_recv[chunk, frame] = tb_send[chunk, frame]

    sattn_pair = remote(sattn.at[1 - core], sattn_peer, pair_ss.at[1], pair_rs.at[1], peer_core)
    left, right = 3 - 2 * core, 1 + 2 * core
    left_y, right_y = {"frame": y_peer(left)}, {"frame": y_peer(right)}
    sy_copies = [
        remote(spart.at[lax.rem(y + 2, 4)], sy_a, ring_ss.at[0], ring_rs.at[0], left_y),
        remote(spart.at[lax.rem(y + right, 4)], sy_b, ring_ss.at[1], ring_rs.at[1], right_y),
        remote(sy_sum, sy_c, ring_ss.at[2], ring_rs.at[2], left_y),
    ]

    temporal_chunk(0)

    own_q.wait()
    each(1, 8, sq_copy, arrive)

    def spatial_pair(i, carry):
        for c in range(2):
            at = pl.ds(pl.multiple_of((2 * i + c) * 128, 128), 128)
            here = pl.ds(pl.multiple_of(i * 128, 128), 128)
            out, dq, dk, dv = attend_pair(sq[0, :, at], sq[1, :, at], sq[2, :, at], sbranch[:, at])
            sattn[c, :, here] = out
            sgrad[0, :, at] = dq.astype(BF16)
            sgrad[1, :, at] = dk.astype(BF16)
            sgrad[2, :, at] = dv.astype(BF16)
        return carry

    lax.fori_loop(0, 4, spatial_pair, 0, unroll=True)
    sattn_pair.start()
    each(1, 8, sb_copy, start)
    own_b = pltpu.make_async_copy(sgrad.at[:, token_rows(token)], sout_hbm.at[:, token], own_sem.at[2])
    own_b.start()

    sg_pair.wait_recv()
    sattn_pair.wait_recv()
    rows_g = jnp.concatenate([sg[...], sg_peer[...]], axis=0)
    rows_o = jnp.concatenate([sattn[core], sattn_peer[...]], axis=0)
    for block in range(4):
        part = rows_dot(rows_g[:, block * 256 : block * 256 + 256], rows_o).astype(BF16)
        for i in range(4):
            spart[i, block * 64 : block * 64 + 64, :] = part[i * 64 : i * 64 + 64]
    sy_copies[0].start()
    sy_copies[1].start()

    each(1, 4, ta_copy, arrive)
    each(1, 4, tf_copy, start)

    temporal_chunk(1)

    sy_copies[0].wait_recv()
    sy_sum[...] = (spart[lax.rem(y + left, 4)].astype(F32) + sy_a[...].astype(F32)).astype(BF16)
    sy_copies[2].start()


    def z_copy(send, recv, ss, rs, d):
        to = lax.rem(zslot + d, 8)
        return remote(send.at[to], recv.at[zslot], ss.at[d], rs.at[d], {"dp": to // 4, "frame": lax.rem(to, 4) * 4 + y})

    def ty_copy(d):
        to = lax.rem(y + d, 4)
        return remote(ty_send.at[to], ty_recv.at[y], ty_ss.at[d], ty_rs.at[d], {"frame": z * 4 + to})

    def sx_copy(d):
        to = lax.rem(x + d, 4)
        return remote(sx_send.at[to], sx_recv.at[x], sx_ss.at[d], sx_rs.at[d], {"token": to * 2 + core})

    def tz_copy(d):
        return z_copy(tz_send, tz_recv, tz_ss, tz_rs, d)

    def sz_copy(d):
        return z_copy(sz_send, sz_recv, sz_ss, sz_rs, d)

    def to_z(landed, send, recv, make, z_make):
        each(1, 4, make, arrive)
        total = jnp.sum(landed[...].astype(F32), axis=0).reshape(4, 64, 128)
        for half in range(2):
            mine = total[:, :, half * 64 : half * 64 + 64]
            send[half * 4 : half * 4 + 4] = jnp.concatenate([mine[:, :32], mine[:, 32:]], axis=2).astype(BF16)
        each(1, 8, z_make, start)
        recv[zslot] = send[zslot]

    def after_z(recv, out, make):
        each(1, 8, make, arrive)
        total = jnp.sum(recv[...].astype(F32), axis=0)
        out[...] = jnp.concatenate([total[:, :64], total[:, 64:]], axis=0)

    each(0, 4, tf_copy, arrive)
    each(1, 8, to_copy, arrive)
    rows_o = tattn_all[...].reshape(1024, 128)
    for block in range(4):
        rows_g = tg_all[:, :, block * 256 : block * 256 + 256].reshape(1024, 256)
        part = rows_dot(rows_o, rows_g).T.astype(BF16)
        for i in range(4):
            ty_send[i, block * 64 : block * 64 + 64, :] = part[i * 64 : i * 64 + 64]
    each(1, 4, ty_copy, start)
    ty_recv[y] = ty_send[y]

    sy_copies[1].wait_recv()
    sy_copies[2].wait_recv()
    total = spart[y].astype(F32) + sy_b[...].astype(F32) + sy_c[...].astype(F32)
    for i in range(4):
        sx_send[i] = total[:, i * 128 : i * 128 + 128].astype(BF16)
    each(1, 4, sx_copy, start)
    sx_recv[x] = sx_send[x]

    to_z(ty_recv, tz_send, tz_recv, ty_copy, tz_copy)
    to_z(sx_recv, sz_send, sz_recv, sx_copy, sz_copy)

    for chunk in range(CHUNKS):
        each(1, 16, lambda d: tb_copy(chunk, d), arrive)
        for a in range(3):
            block = tb_recv[chunk, :, a * 16 : a * 16 + 16, :].astype(F32).reshape(16, 2, 8, 256)
            for half in range(2):
                rows = rows_dot(shuffle, block[:, half].reshape(128, 256).astype(BF16)).astype(BF16)
                for i in range(2):
                    at = (2 * (2 * half + i) + chunk) * 128
                    tout[a, :, :, at : at + 128] = rows[:, i * 128 : i * 128 + 128].reshape(8, 16, 128)
    store = pltpu.make_async_copy(tout, tout_hbm, out_sem)
    store.start()

    after_z(sz_recv, sproj_out, sz_copy)
    after_z(tz_recv, tproj_out, tz_copy)

    each(1, 8, sb_copy, arrive)
    each(1, 16, tg_copy, leave)
    for chunk in range(CHUNKS):
        each(1, 16, lambda d: tc_copy(chunk, d), leave)
        each(1, 16, lambda d: tb_copy(chunk, d), leave)
    each(1, 8, sg_copy, leave)
    each(1, 8, sq_copy, leave)
    each(1, 8, sb_copy, leave)
    each(1, 4, sx_copy, leave)
    each(1, 4, ta_copy, leave)
    each(0, 4, tf_copy, leave)
    each(1, 8, to_copy, leave)
    each(1, 4, ty_copy, leave)
    each(1, 8, sz_copy, leave)
    each(1, 8, tz_copy, leave)
    for copy in [sg_pair, sattn_pair] + sy_copies:
        copy.wait_send()
    own_b.wait()
    store.wait()


def local(temporal_qkv, spatial_qkv, out_grad, temporal_proj, spatial_proj):
    def vm(*shape):
        return pltpu.VMEM(shape, BF16)

    def dma(*shape):
        return pltpu.SemaphoreType.DMA(shape)

    any_spec = pl.BlockSpec(memory_space=pl.ANY)
    vmem_spec = pl.BlockSpec(memory_space=pltpu.VMEM)
    tout, sout, tproj, sproj = pl.pallas_call(
        body,
        out_shape=(
            jax.ShapeDtypeStruct((3, 8, 16, 1024), BF16),
            jax.ShapeDtypeStruct((3, 8, 16, 1024), BF16),
            jax.ShapeDtypeStruct((64, 64), F32),
            jax.ShapeDtypeStruct((64, 64), F32),
        ),
        in_specs=[any_spec] * 5,
        out_specs=(any_spec, any_spec, vmem_spec, vmem_spec),
        scratch_shapes=[
            vm(3, 8, 16, 1024), vm(8, 16, 1024), vm(1024, 1024), vm(1024, 1024),
            vm(16, 16, 512), vm(16, 16, 512), vm(2, 16, 48, 256), vm(2, 16, 48, 256),
            vm(8, 128, 1024), vm(128, 1024), vm(3, 128, 512), pltpu.VMEM((3, 128, 512), F32),
            vm(2, 16, 48, 256), vm(2, 16, 48, 256), vm(3, 8, 16, 1024), vm(8, 128, 128),
            vm(128, 1024), vm(3, 128, 1024), vm(128, 1024), vm(3, 128, 1024), vm(2, 128, 512),
            vm(8, 128, 128), vm(128, 1024), vm(128, 512),
            vm(4, 256, 128), vm(4, 256, 128), vm(8, 32, 128), vm(8, 32, 128),
            vm(4, 256, 512), vm(256, 512), vm(256, 512), vm(256, 512), vm(256, 512),
            vm(4, 256, 128), vm(4, 256, 128), vm(8, 32, 128), vm(8, 32, 128),
            dma(4), dma(16), dma(16), dma(2, 16), dma(2, 16), dma(2, 16), dma(2, 16),
            dma(8), dma(8), dma(8), dma(8), dma(8), dma(8), dma(3),
            dma(2), dma(2), dma(4), dma(4), dma(4), dma(4), dma(8), dma(8), dma(3), dma(3), dma(4), dma(4), dma(4), dma(4),
            dma(8), dma(8), dma(8), dma(8), pltpu.SemaphoreType.DMA,
        ],
        compiler_params=pltpu.CompilerParams(
            collective_id=0, has_side_effects=True, vmem_limit_bytes=60 * 1024 * 1024
        ),
    )(
        temporal_qkv.reshape(3, 8, 16, 1024),
        spatial_qkv.reshape(3, 8, 16, 1024),
        out_grad.reshape(8, 16, 1024),
        temporal_proj,
        spatial_proj,
    )
    shape = (3, 1, 8, 16, 1024)
    return tout.reshape(shape), sout.reshape(shape), tproj, sproj


def solution(mesh):
    in_specs = (
        P(None, "dp", "frame", "token", None),
        P(None, "dp", "frame", "token", None),
        P("dp", "frame", "token", None),
        P(),
        P(),
    )
    out_specs = (
        P(None, "dp", "frame", "token", None),
        P(None, "dp", "frame", "token", None),
        P("frame", ("token", "dp")),
        P("frame", ("token", "dp")),
    )
    return jax.shard_map(local, mesh=mesh, in_specs=in_specs, out_specs=out_specs, check_vma=False)
```

time: 84.9 us -> 78.2 us (0.921)
  local copies, waits for them, and re-layouts: 7.79 us -> 4.28 us
  Pallas kernels: 76.2 us -> 73.2 us
    unnamed x12 -> x10, local copies, waits for them, and re-layouts: 7.79 us -> 4.28 us
    pallas_call x1, Pallas kernels: 76.2 us -> 73.2 us  [local(): pl.pallas_call(body, out_shape=(jax.ShapeDtypeStruct((3, 8, 16, 1024), BF...]
where the time goes in v3:
time: 78.2 us; the launch traced here: 78.1 us
  Pallas kernels  73.2 us (94%)
  local copies, waits for them, and re-layouts  4.28 us (5%)
    pallas_call x1, Pallas kernels, local(): pl.pallas_call(body, out_shape=(jax.ShapeDtypeStruct((3, 8, 16, 1024), BF...  73.2 us
    unnamed x10, local copies, waits for them, and re-layouts  4.28 us

profile of v3, /device:TPU:8, one launch (start us, length us, event | category | flops | bytes accessed | tf_op | source)
XLA Modules:
  0.0 78.1 jit_solution(12128084373367692422)
XLA Ops:
  0.6 73.2 %shard_map.84 = (bf16[3,8,16,1024]{3,2,1,0:T(8,128)(2,1)}, bf16[3,8,16,1024]{3,2,1,0:T(8,128)(2,1)}, f32[64,64]{1,0:T(8,128)}, f32[64,64]{1,0:T(8,128)}) custom-call(bf16[3,8,16,1024]{3,2,1,0:T(8,128)(2,1)} %bitcast.11, bf16[3,8,16,1024]{3,2,1,0:T(8,128)(2,1)} %bitcast.12, bf16[8,16,1024]{2,1,0:T(8,128)(2,1)} %bitcast.13, bf16[1024,1024]{1,0:T(8,128)(2,1)} %tproj_hbm.1, ...), custom_call_target="tpu_custom_call" | custom-call | tf_op jit(solution)/shard_map/pallas_call | solution.py:420
  73.8 0.0 copy-start
  73.8 0.0 copy-start.2
  73.8 0.0 copy-start.1
  73.8 2.2 %copy.15 = bf16[3,1,8,16,1024]{4,3,2,1,0:T(8,128)(2,1)} copy(bf16[3,1,8,16,1024]{4,3,2,1,0:T(8,128)(2,1)} %bitcast.10) | data formatting | bytes 1572864
  76.0 0.0 copy-done
  76.0 0.9 %copy.16 = bf16[3,1,8,16,1024]{4,3,2,1,0:T(8,128)(2,1)} copy(bf16[3,1,8,16,1024]{4,3,2,1,0:T(8,128)(2,1)S(1)} %bitcast.9) | data formatting | bytes 1572864
  76.9 0.0 copy-done.2
  76.9 0.6 copy.17
  77.5 0.0 copy-done.1
  77.5 0.6 copy.18
Async XLA Ops:
  73.8 2.2 %copy-start = (bf16[3,8,16,1024]{3,2,1,0:T(8,128)(2,1)S(1)}, bf16[3,8,16,1024]{3,2,1,0:T(8,128)(2,1)}, u32[]{:S(2)}) copy-start(bf16[3,8,16,1024]{3,2,1,0:T(8,128)(2,1)} %get-tuple-element.9) | copy-start | bytes 2359300
  73.8 3.1 %copy-start.2 = (f32[64,64]{1,0:T(8,128)S(1)}, f32[64,64]{1,0:T(8,128)}, u32[]{:S(2)}) copy-start(f32[64,64]{1,0:T(8,128)} %get-tuple-element.22) | copy-start | bytes 49156
  73.8 3.7 %copy-start.1 = (f32[64,64]{1,0:T(8,128)S(1)}, f32[64,64]{1,0:T(8,128)}, u32[]{:S(2)}) copy-start(f32[64,64]{1,0:T(8,128)} %get-tuple-element.23) | copy-start | bytes 49156

commit v4 on v3

--- a/solution.py
+++ b/solution.py
@@ -195,7 +195,6 @@
         copy.wait_send()
 
     each(1, 16, tg_copy, start)
-    each(1, 16, lambda d: tc_copy(0, d), start)
     each(1, 8, sg_copy, start)
     own_g = pltpu.make_async_copy(grad_hbm.at[token], sg.at[token_rows(token)], own_sem.at[0])
     own_q = pltpu.make_async_copy(squkv_hbm.at[:, token], sq.at[:, token_rows(token)], own_sem.at[1])
@@ -203,6 +202,7 @@
     own_q.start()
     each(1, 8, sq_copy, start)
 
+    each(1, 16, lambda d: tc_copy(0, d), start)
     each(1, 16, lambda d: tc_copy(1, d), start)
 
     peer_core = {"token": token + 1 - 2 * core}

time: 78.2 us -> 78.2 us (level)
  no operation moved by 1% of the time
where the time goes in v4:
time: 78.2 us; the launch traced here: 78.1 us
  Pallas kernels  73.2 us (94%)
  local copies, waits for them, and re-layouts  4.28 us (5%)
    pallas_call x1, Pallas kernels, local(): pl.pallas_call(body, out_shape=(jax.ShapeDtypeStruct((3, 8, 16, 1024), BF...  73.2 us
    unnamed x10, local copies, waits for them, and re-layouts  4.28 us

profile of v4, /device:TPU:8, one launch (start us, length us, event | category | flops | bytes accessed | tf_op | source)
XLA Modules:
  0.0 78.1 jit_solution(15788597701712285840)
XLA Ops:
  0.6 73.2 %shard_map.84 = (bf16[3,8,16,1024]{3,2,1,0:T(8,128)(2,1)}, bf16[3,8,16,1024]{3,2,1,0:T(8,128)(2,1)}, f32[64,64]{1,0:T(8,128)}, f32[64,64]{1,0:T(8,128)}) custom-call(bf16[3,8,16,1024]{3,2,1,0:T(8,128)(2,1)} %bitcast.11, bf16[3,8,16,1024]{3,2,1,0:T(8,128)(2,1)} %bitcast.12, bf16[8,16,1024]{2,1,0:T(8,128)(2,1)} %bitcast.13, bf16[1024,1024]{1,0:T(8,128)(2,1)} %tproj_hbm.1, ...), custom_call_target="tpu_custom_call" | custom-call | tf_op jit(solution)/shard_map/pallas_call | solution.py:420
  73.8 0.0 copy-start
  73.8 0.0 copy-start.2
  73.8 0.0 copy-start.1
  73.8 2.2 %copy.15 = bf16[3,1,8,16,1024]{4,3,2,1,0:T(8,128)(2,1)} copy(bf16[3,1,8,16,1024]{4,3,2,1,0:T(8,128)(2,1)} %bitcast.10) | data formatting | bytes 1572864
  76.0 0.0 copy-done
  76.0 0.9 %copy.16 = bf16[3,1,8,16,1024]{4,3,2,1,0:T(8,128)(2,1)} copy(bf16[3,1,8,16,1024]{4,3,2,1,0:T(8,128)(2,1)S(1)} %bitcast.9) | data formatting | bytes 1572864
  76.9 0.0 copy-done.2
  76.9 0.6 copy.17
  77.5 0.0 copy-done.1
  77.5 0.6 copy.18
Async XLA Ops:
  73.8 2.2 %copy-start = (bf16[3,8,16,1024]{3,2,1,0:T(8,128)(2,1)S(1)}, bf16[3,8,16,1024]{3,2,1,0:T(8,128)(2,1)}, u32[]{:S(2)}) copy-start(bf16[3,8,16,1024]{3,2,1,0:T(8,128)(2,1)} %get-tuple-element.9) | copy-start | bytes 2359300
  73.8 3.1 %copy-start.2 = (f32[64,64]{1,0:T(8,128)S(1)}, f32[64,64]{1,0:T(8,128)}, u32[]{:S(2)}) copy-start(f32[64,64]{1,0:T(8,128)} %get-tuple-element.22) | copy-start | bytes 49156
  73.8 3.7 %copy-start.1 = (f32[64,64]{1,0:T(8,128)S(1)}, f32[64,64]{1,0:T(8,128)}, u32[]{:S(2)}) copy-start(f32[64,64]{1,0:T(8,128)} %get-tuple-element.23) | copy-start | bytes 49156
